TPU v7x, 32 devices: a whole 2x2x4 slice. The times are simulated.
32 devices in a mesh: dp: 8 (over z, core), tensor: 4 (over y, x).
Axes of the slice: x: 2, y: 2, z: 4, core: 2. Of those that a mesh axis runs over, the one named last changes fastest.
Arguments:
- tokens: bfloat16 [4096, 2048], P(('dp', 'tensor')), may hold values from -6 to 6
- lengths: int32 [8, 8], P('dp'), may hold values from 1 to 128, 512 in all within a row
- group_prefix: int32 [8], replicated, may hold values from 0 to 7, as said below
- prefix_cache: bfloat16 [32768, 512], P(('dp', 'tensor')), may hold values from -340 to 340
- query_weight: bfloat16 [2048, 1024], P(None, 'tensor'), may hold values from -0.125 to 0.125
- key_weight: bfloat16 [2048, 256], replicated, may hold values from -0.375 to 0.375
- value_weight: bfloat16 [2048, 256], replicated, may hold values from -0.125 to 0.125
- out_weight: bfloat16 [1024, 2048], P('tensor'), may hold values from -0.1875 to 0.1875
- gate_up_weight: bfloat16 [2, 2048, 5120], P(None, None, 'tensor'), may hold values from -0.125 to 0.125
- down_weight: bfloat16 [5120, 2048], P('tensor'), may hold values from -0.078125 to 0.078125
Outputs:
- layer_out: bfloat16 [4096, 2048], P(('dp', 'tensor'))
Inputs may be any that keep to these rules, and one draw needn't show every extreme that they name: The 8 lengths of a group sum to 512, and one of them is exactly 128. `group_prefix`: several groups may continue the same slot.
All inputs are finite; a program needn't handle non-finite values.
Results may differ from a plain program's by a relative error of at most 0.023.
Values may be sent and summed in bfloat16 or wider, within the bound.
A program may use at most 128 MiB of HBM per device.

v0:
```python
import math

import jax
import jax.numpy as jnp
from jax import lax
from jax.sharding import PartitionSpec as P

QH = 16
KVH = 4
HD = 64
PLEN = 4096


NEG_FILL = -1e30


def token_layout(lengths, total_rows):
    ends_at = jnp.cumsum(lengths)
    starts_at = ends_at - lengths
    indices = jnp.arange(total_rows, dtype=jnp.int32)
    request = jnp.sum((indices[:, None] >= ends_at[None, :]).astype(jnp.int32), axis=1)
    begins = jnp.max(
        jnp.where(starts_at[None, :] <= indices[:, None], starts_at[None, :], 0), axis=1
    )
    return ((PLEN + indices - begins).astype(jnp.float32), request)


def rope_tables(positions):
    halves = HD // 2
    steps_float = jnp.arange(halves, dtype=jnp.float32)
    inverse = jnp.exp(steps_float * (-2.0 * math.log(10000.0) / HD))
    angles = positions[:, None] * inverse[None, :]
    return (jnp.cos(angles), jnp.sin(angles))


def rotate(values, cos_table, sin_table):
    halves = values.shape[-1] // 2
    former = values[..., :halves]
    latter = values[..., halves:]
    cos_rows = cos_table[:, None, :]
    sin_rows = sin_table[:, None, :]
    return jnp.concatenate(
        [former * cos_rows - latter * sin_rows, latter * cos_rows + former * sin_rows], axis=-1
    )


def norm_rows(inputs):
    floats = inputs.astype(jnp.float32)
    return (floats * lax.rsqrt(jnp.mean(floats * floats, axis=-1, keepdims=True) + 1e-05)).astype(
        jnp.bfloat16
    )


def softmax_block(queries, keys_block, values_block, scaling, allowed):
    scores = (
        jnp.einsum("thd,nhd->thn", queries, keys_block, preferred_element_type=jnp.float32)
        * scaling
    )
    if allowed is not None:
        scores = jnp.where(allowed, scores, NEG_FILL)
    top_score = jnp.max(scores, axis=2)
    exponent = jnp.exp(scores - top_score[:, :, None])
    weight = jnp.sum(exponent, axis=2)
    blended = jnp.einsum(
        "thn,nhd->thd",
        exponent.astype(jnp.bfloat16),
        values_block,
        preferred_element_type=jnp.float32,
    )
    return (top_score, weight, blended)


def merge_states(former, latter):
    top_one, weight_one, blend_one = former
    top_two, weight_two, blend_two = latter
    overall = jnp.maximum(top_one, top_two)
    factor_one = jnp.exp(top_one - overall)
    factor_two = jnp.exp(top_two - overall)
    return (
        overall,
        weight_one * factor_one + weight_two * factor_two,
        blend_one * factor_one[:, :, None] + blend_two * factor_two[:, :, None],
    )


def on_device(
    tokens,
    lengths,
    group_prefix,
    prefix_cache,
    query_weight,
    key_weight,
    value_weight,
    out_weight,
    gate_up_weight,
    down_weight,
):
    tensor_count = lax.axis_size("tensor")
    tensor_rank = lax.axis_index("tensor")
    group_rank = lax.axis_index("dp")
    row_count = tokens.shape[0]
    group_tokens = row_count * tensor_count
    local_heads = query_weight.shape[1] // HD
    head_ratio = QH // KVH
    local_kv = max(1, local_heads // head_ratio)
    repeat_by = local_heads // local_kv
    kv_first = tensor_rank * local_heads // head_ratio
    kv_total = KVH * HD
    query_width = local_heads * HD
    kv_width = local_kv * HD
    scaling = 1.0 / math.sqrt(HD)
    positions, request = token_layout(lengths[0], group_tokens)
    cos_table, sin_table = rope_tables(positions)
    key_cols = lax.dynamic_slice_in_dim(key_weight, kv_first * HD, kv_width, 1)
    value_cols = lax.dynamic_slice_in_dim(value_weight, kv_first * HD, kv_width, 1)
    projection = jnp.concatenate([query_weight, key_cols, value_cols], axis=1)
    normed = norm_rows(tokens)
    segment = lax.all_gather(normed, "tensor", axis=0, tiled=True)
    seg_rows = segment.shape[0]
    mapped = jnp.dot(segment, projection, preferred_element_type=jnp.float32)
    query_part = rotate(
        mapped[:, :query_width].reshape(seg_rows, local_heads, HD), cos_table, sin_table
    )
    key_part = rotate(
        mapped[:, query_width : query_width + kv_width].reshape(seg_rows, local_kv, HD),
        cos_table,
        sin_table,
    )
    projected = jnp.concatenate(
        [
            query_part.reshape(seg_rows, query_width),
            key_part.reshape(seg_rows, kv_width),
            mapped[:, query_width + kv_width :],
        ],
        axis=1,
    ).astype(jnp.bfloat16)
    queries = projected[:, :query_width].reshape(group_tokens, local_heads, HD)
    own_keys = jnp.repeat(
        projected[:, query_width : query_width + kv_width].reshape(group_tokens, local_kv, HD),
        repeat_by,
        axis=1,
    )
    own_values = jnp.repeat(
        projected[:, query_width + kv_width :].reshape(group_tokens, local_kv, HD),
        repeat_by,
        axis=1,
    )
    slot_wanted = group_prefix[group_rank]
    shard_rows = prefix_cache.shape[0]
    segment = lax.all_gather(prefix_cache, "dp", axis=0, tiled=True)
    seg_rows = segment.shape[0]
    indices = jnp.arange(seg_rows, dtype=jnp.int32)
    matches = indices // shard_rows == slot_wanted
    places = indices % shard_rows
    chosen = (
        jnp.zeros_like(prefix_cache)
        .at[places]
        .add(jnp.where(matches[:, None], segment, jnp.zeros_like(segment)))
    )
    start_state = (
        jnp.full((group_tokens, local_heads), NEG_FILL, jnp.float32),
        jnp.zeros((group_tokens, local_heads), jnp.float32),
        jnp.zeros((group_tokens, local_heads, HD), jnp.float32),
    )
    segment = lax.all_gather(chosen, "tensor", axis=0, tiled=True)
    seg_rows = segment.shape[0]
    keys_block = lax.dynamic_slice_in_dim(segment, kv_first * HD, kv_width, 1).reshape(
        seg_rows, local_kv, HD
    )
    values_block = lax.dynamic_slice_in_dim(segment, kv_total + kv_first * HD, kv_width, 1).reshape(
        seg_rows, local_kv, HD
    )
    keys_block = jnp.repeat(keys_block, repeat_by, axis=1)
    values_block = jnp.repeat(values_block, repeat_by, axis=1)
    prefix_state = merge_states(
        start_state, softmax_block(queries, keys_block, values_block, scaling, None)
    )
    indices = jnp.arange(group_tokens, dtype=jnp.int32)
    allowed = (request[:, None] == request[None, :]) & (indices[None, :] <= indices[:, None])
    suffix_state = softmax_block(queries, own_keys, own_values, scaling, allowed[:, None, :])
    top_score, weight, blended = merge_states(prefix_state, suffix_state)
    attended = (
        (blended / weight[:, :, None]).astype(jnp.bfloat16).reshape(group_tokens, query_width)
    )
    attn_sum = lax.psum_scatter(
        jnp.dot(attended, out_weight, preferred_element_type=jnp.float32).astype(jnp.bfloat16),
        "tensor",
        scatter_dimension=0,
        tiled=True,
    ).astype(jnp.float32)
    middle = (tokens.astype(jnp.float32) + attn_sum).astype(jnp.bfloat16)
    segment = lax.all_gather(norm_rows(middle), "tensor", axis=0, tiled=True)
    gate_value = jnp.dot(segment, gate_up_weight[0], preferred_element_type=jnp.float32)
    upward = jnp.dot(segment, gate_up_weight[1], preferred_element_type=jnp.float32)
    hidden = (jax.nn.silu(gate_value) * upward).astype(jnp.bfloat16)
    ffn_sum = lax.psum_scatter(
        jnp.dot(hidden, down_weight, preferred_element_type=jnp.float32).astype(jnp.bfloat16),
        "tensor",
        scatter_dimension=0,
        tiled=True,
    ).astype(jnp.float32)
    return (middle.astype(jnp.float32) + ffn_sum).astype(jnp.bfloat16)


def solution(mesh):
    return jax.shard_map(
        on_device,
        mesh=mesh,
        in_specs=(
            P(("dp", "tensor"), None),
            P("dp", None),
            P(),
            P(("dp", "tensor"), None),
            P(None, "tensor"),
            P(),
            P(),
            P("tensor", None),
            P(None, None, "tensor"),
            P("tensor", None),
        ),
        out_specs=P(("dp", "tensor"), None),
        check_vma=False,
    )
```

profile of v0, /device:TPU:0, one launch (start us, length us, event | category | flops | bytes accessed | tf_op | source)
XLA Modules:
  0.0 389.4 jit_solution(12167642294804940892)
XLA Ops:
  6.5 0.0 copy-start
  6.5 0.0 all-gather.5.cloned.1.call-start
  6.5 0.7 all-gather.5.cloned.1.call-update
  7.3 0.0 all-gather.9.cloned.1.call-start
  7.3 1.2 fusion.56
  8.5 2.0 fusion.57
  10.5 0.0 all-gather.9.cloned.1.call-update
  10.6 0.0 all-gather.7.cloned.1.call-start
  10.6 1.3 dynamic_slice.15
  11.9 0.7 fusion.84
  12.6 81.1 %all-gather.5.cloned.1.call-done = bf16[8192,512]{1,0:T(8,128)(2,1)} async-done(((bf16[1024,512]{1,0:T(8,128)(2,1)}), bf16[8192,512]{1,0:T(8,128)(2,1)}) %all-gather.5.cloned.1.call-update) | async-done | bytes 8388624 | tf_op jit(solution)/shard_map/all_gather | solution.py:150
  93.8 0.0 copy-start.7
  93.8 54.9 %scatter_custom_fusion = bf16[1024,512]{1,0:T(8,128)(2,1)} fusion(s32[8192]{0:T(1024)S(1)} %bitcast.91, bf16[8192,512]{1,0:T(8,128)(2,1)} %all-gather.5.cloned.1.call-done, pred[8192]{0:T(1024)(128)(4,1)S(1)} %fusion.84, bf16[]{:T(256)} %constant.73.clone.1), kind=kCustom, calls=%fused_computation.7 | custom fusion | flops 8388608 | bytes 9446400 | tf_op jit(solution)/shard_map/scatter-add | solution.py:158
  148.7 0.0 all-gather.7.cloned.1.call-update
  148.7 0.0 reduce-scatter.3.cloned.1.call-start
  148.8 0.0 copy-done.7
  148.8 0.2 reduce-window.4
  149.0 0.1 select_reduce_fusion
  149.1 0.1 convert_reduce_fusion
  149.2 0.3 multiply_cosine_fusion.1
  149.5 0.2 fusion.65
  149.7 1.6 constant_dynamic-slice_fusion.1
  151.3 0.0 all-gather.9.cloned.1.call-done
  151.3 3.3 fusion.27
  154.6 0.6 slice.71
  155.3 0.3 fusion.81
  155.7 0.1 subtract_convert_fusion
  155.7 0.0 copy-start.5
  155.8 0.6 copy-done.5
  156.4 0.9 fusion.20
  157.3 0.0 copy-start.3
  157.3 2.0 copy-done.3
  159.3 0.9 fusion.15
  160.3 39.9 %all-gather.7.cloned.1.call-done = bf16[4096,512]{1,0:T(8,128)(2,1)} async-done(((bf16[1024,512]{1,0:T(8,128)(2,1)}), bf16[4096,512]{1,0:T(8,128)(2,1)}) %all-gather.7.cloned.1.call-update) | async-done | bytes 4194320 | tf_op jit(solution)/shard_map/all_gather | solution.py:165
  200.1 3.2 constant_dynamic-slice_fusion
  203.3 1.5 copy.18
  204.8 0.3 copy.17
  205.2 14.3 %bitcast_reduce_fusion = (f32[512,4]{0,1:T(4,128)S(1)}, f32[4,4096,512]{2,1,0:T(8,128)}) fusion(bf16[512,4,32]{0,2,1:T(8,128)(2,1)} %copy-done.5, bf16[512,4,32]{0,2,1:T(8,128)(2,1)S(1)} %get-tuple-element.10, bf16[4096,64]{0,1:T(8,128)(2,1)S(1)} %copy.17), kind=kOutput, calls=%fused_computation.2 | convolution fusion | flops 1091041280 | bytes 34349056 | tf_op jit(solution)/shard_map/thd,nhd->thn/dot_general | solution.py:56
  219.4 13.8 %fusion.1 = f32[512,4]{0,1:T(4,128)S(1)} fusion(f32[4,4096,512]{2,1,0:T(8,128)} %get-tuple-element.19, f32[512,4]{0,1:T(4,128)S(1)} %get-tuple-element.18), kind=kLoop, calls=%fused_computation.4 | loop fusion | flops 25163776 | bytes 33570816 | tf_op jit(solution)/shard_map/reduce_sum | solution.py:63
  233.2 0.0 copy-start.4
  233.2 0.0 copy-start.6
  233.3 13.6 %fusion.53 = f32[512,4,64]{0,2,1:T(8,128)S(1)} fusion(f32[4,4096,512]{2,1,0:T(8,128)} %get-tuple-element.19, f32[512,4]{0,1:T(4,128)S(1)} %get-tuple-element.18, bf16[4096,64]{0,1:T(8,128)(2,1)S(1)} %copy.18, f32[512,4]{0,1:T(4,128)S(1)} %get-tuple-element.7, f32[512,4]{0,1:T(4,128)S(1)} %get-tuple-element.15, f32[512,4]{0,1:T(4,128)S(1)} %get-tuple-element.14), kind=kOutput, calls=%fused_computation.46 | convolution fusion | flops 1099300864 | bytes 34635776 | tf_op jit(solution)/shard_map/thn,nhd->thd/dot_general | solution.py:64
  246.9 0.0 copy-done.4
  246.9 0.0 copy-done.6
  246.9 1.3 fusion.69
  248.2 0.0 copy-start.1
  248.2 0.0 copy-done
  248.2 2.1 convolution_convert_fusion
  250.3 0.0 reduce-scatter.3.cloned.1.call-update
  250.3 0.0 all-gather.11.cloned.1.call-start
  250.4 35.3 %reduce-scatter.3.cloned.1.call-done = bf16[128,2048]{1,0:T(8,128)(2,1)} async-done(((bf16[512,2048]{1,0:T(8,128)(2,1)}), bf16[128,2048]{1,0:T(8,128)(2,1)}) %reduce-scatter.3.cloned.1.call-update) | async-done | bytes 524304 | tf_op jit(solution)/shard_map/reduce_scatter | solution.py:185
  285.7 0.0 copy-done.1
  285.7 1.3 fusion.59
  287.0 2.0 fusion.60
  289.0 0.0 all-gather.11.cloned.1.call-update
  289.0 0.3 reduce-scatter.5.cloned.1.call-start
  289.3 35.2 %all-gather.11.cloned.1.call-done = bf16[512,2048]{1,0:T(8,128)(2,1)} async-done(((bf16[128,2048]{1,0:T(8,128)(2,1)}), bf16[512,2048]{1,0:T(8,128)(2,1)}) %all-gather.11.cloned.1.call-update) | async-done | bytes 2097168 | tf_op jit(solution)/shard_map/all_gather | solution.py:192
  324.5 7.5 %fusion.10 = f32[512,1280]{1,0:T(8,128)} fusion(bf16[512,2048]{1,0:T(8,128)(2,1)} %all-gather.11.cloned.1.call-done, bf16[2,2048,1280]{2,1,0:T(8,128)(2,1)} %param.18), kind=kOutput, calls=%fused_computation.12 | convolution fusion | flops 2684354560 | bytes 9961472 | tf_op jit(solution)/shard_map/dot_general | solution.py:193
  332.0 0.0 copy-start.2
  332.0 13.1 %convolution_convert_fusion.1 = bf16[512,2048]{1,0:T(8,128)(2,1)} fusion(bf16[1280,2048]{1,0:T(8,128)(2,1)} %param.19, bf16[512,2048]{1,0:T(8,128)(2,1)} %all-gather.11.cloned.1.call-done, bf16[2,2048,1280]{2,1,0:T(8,128)(2,1)} %param.18, f32[512,1280]{1,0:T(8,128)} %fusion.10), kind=kOutput, calls=%fused_computation.25 | convolution fusion | flops 5373689856 | bytes 17301504 | tf_op jit(solution)/shard_map/dot_general | solution.py:197
  345.1 0.0 reduce-scatter.5.cloned.1.call-update
  345.1 35.4 %reduce-scatter.5.cloned.1.call-done = bf16[128,2048]{1,0:T(8,128)(2,1)} async-done(((bf16[512,2048]{1,0:T(8,128)(2,1)}), bf16[128,2048]{1,0:T(8,128)(2,1)}) %reduce-scatter.5.cloned.1.call-update) | async-done | bytes 524304 | tf_op jit(solution)/shard_map/reduce_scatter | solution.py:196
  380.5 0.0 copy-done.2
  380.5 2.1 fusion.61
  (10 shorter events, 0.1 us)
Async XLA Ops:
  6.5 241.7 %copy-start = (bf16[256,2048]{1,0:T(8,128)(2,1)S(1)}, bf16[256,2048]{1,0:T(8,128)(2,1)}, u32[]{:S(2)}) copy-start(bf16[256,2048]{1,0:T(8,128)(2,1)} %param.17) | copy-start | bytes 3145732
  6.5 87.2 %all-gather.5.cloned.1.call-start = ((), (), s32[]{:S(2)}) async-start(), calls=%async_computation.2 | async-start | bytes 9437184 | tf_op jit(solution)/shard_map/all_gather | solution.py:150
  7.3 144.0 %all-gather.9.cloned.1.call-start = ((), (), s32[]{:S(2)}) async-start(), calls=%async_computation.4 | async-start | bytes 2621440 | tf_op jit(solution)/shard_map/all_gather | solution.py:118
  10.6 189.5 %all-gather.7.cloned.1.call-start = ((), (), s32[]{:S(2)}) async-start(), calls=%async_computation.3 | async-start | bytes 5242880 | tf_op jit(solution)/shard_map/all_gather | solution.py:165
  93.8 55.0 %copy-start.7 = (s32[1,8]{1,0:T(1,128)S(1)}, s32[1,8]{1,0:T(1,128)}, u32[]{:S(2)}) copy-start(s32[1,8]{1,0:T(1,128)} %param.11) | copy-start | bytes 100
  148.7 137.0 %reduce-scatter.3.cloned.1.call-start = ((), (), s32[]{:S(2)}) async-start(), calls=%async_computation.5 | async-start | bytes 2621440 | tf_op jit(solution)/shard_map/reduce_scatter | solution.py:185
  155.7 0.7 copy-start.5
  157.3 2.0 copy-start.3
  233.2 13.6 %copy-start.4 = (f32[4,512,512]{2,1,0:T(8,128)S(1)}, f32[4,512,512]{2,1,0:T(8,128)}, u32[]{:S(2)}) copy-start(f32[4,512,512]{2,1,0:T(8,128)} %copy-done.3) | copy-start | bytes 12582916
  233.2 13.6 %copy-start.6 = (bf16[512,64]{0,1:T(8,128)(2,1)S(1)}, bf16[512,64]{0,1:T(8,128)(2,1)}, u32[]{:S(2)}) copy-start(bf16[512,64]{0,1:T(8,128)(2,1)} %slice.71) | copy-start | bytes 196612
  248.2 37.5 %copy-start.1 = (bf16[128,2048]{1,0:T(8,128)(2,1)S(1)}, bf16[128,2048]{1,0:T(8,128)(2,1)}, u32[]{:S(2)}) copy-start(bf16[128,2048]{1,0:T(8,128)(2,1)} %param.10) | copy-start | bytes 1572868
  250.3 74.2 %all-gather.11.cloned.1.call-start = ((), (), s32[]{:S(2)}) async-start(), calls=%async_computation.6 | async-start | bytes 2621440 | tf_op jit(solution)/shard_map/all_gather | solution.py:192
  289.0 91.5 %reduce-scatter.5.cloned.1.call-start = ((), (), s32[]{:S(2)}) async-start(), calls=%async_computation.7 | async-start | bytes 2621440 | tf_op jit(solution)/shard_map/reduce_scatter | solution.py:196
  332.0 48.5 %copy-start.2 = (bf16[128,2048]{1,0:T(8,128)(2,1)S(1)}, bf16[128,2048]{1,0:T(8,128)(2,1)}, u32[]{:S(2)}) copy-start(bf16[128,2048]{1,0:T(8,128)(2,1)} %reduce-scatter.3.cloned.1.call-done) | copy-start | bytes 1572868
Sparse Core Ops, SparseCore 0:
  9.0 84.7 all-gather.4
  95.6 33.8 all-gather.8
  148.8 51.2 all-gather.6
  250.4 35.1 reduce-scatter.2
  289.1 35.2 all-gather.10
  345.3 35.1 reduce-scatter.4
where the time goes:
time: 390 us; the launch traced here: 389 us
  waiting for transfers between devices  228 us (58%)
  other arithmetic  80.3 us (21%)
  matrix products  56.1 us (14%)
  between operations  13.7 us (4%)
  local copies, waits for them, and re-layouts  11.3 us (3%)
    all_gather x1, waiting for transfers between devices, on_device(): segment = lax.all_gather(prefix_cache, 'dp', axis=0, tiled=True)  81.1 us
    scatter-add x1, other arithmetic, on_device(): chosen = jnp.zeros_like(prefix_cache).at[places].add(jnp.where(matches[:,...  54.9 us
    all_gather x1, waiting for transfers between devices, on_device(): segment = lax.all_gather(chosen, 'tensor', axis=0, tiled=True)  39.9 us
    reduce_scatter x1, waiting for transfers between devices, on_device(): lax.psum_scatter(jnp.dot(hidden, down_weight, preferred_element_type=jnp....  35.4 us
    reduce_scatter x1, waiting for transfers between devices, on_device(): lax.psum_scatter(jnp.dot(attended, out_weight, preferred_element_type=jnp...  35.3 us
    all_gather x1, waiting for transfers between devices, on_device(): segment = lax.all_gather(norm_rows(middle), 'tensor', axis=0, tiled=True)  35.2 us
    dot_general x2, matrix products, softmax_block(): jnp.einsum('thd,nhd->thn', queries, keys_block, preferred_element_type=jn...  15.2 us
    dot_general x2, matrix products, softmax_block(): jnp.einsum('thn,nhd->thd', exponent.astype(jnp.bfloat16), values_block, p...  14.9 us
  transfers between devices with their start and end apart: 6, of which 5 were waited for; matrix products, arithmetic and copies ran while one was open for 18% of the time, Pallas kernels for 0%

commit v1 on v0

v1 whole, which is shorter than its diff:
```python
import functools
import math

import jax
import jax.numpy as jnp
from jax import lax
from jax.experimental import pallas as pl
from jax.experimental.pallas import tpu as pltpu
from jax.sharding import PartitionSpec as P

QH = 16
KVH = 4
HD = 64
PLEN = 4096
LANES = 128
NEG_FILL = -1e30
VMEM = pl.BlockSpec(memory_space=pltpu.VMEM)
SMEM = pl.BlockSpec(memory_space=pltpu.SMEM)
ANY = pl.BlockSpec(memory_space=pl.ANY)
MESH = pl.DeviceIdType.MESH
BF16 = jnp.bfloat16
F32 = jnp.float32
MIB = 1 << 20


def norm_rows(inputs):
    floats = inputs.astype(F32)
    mean = jnp.mean(floats * floats, axis=-1, keepdims=True)
    return (floats * lax.rsqrt(mean + 1e-05)).astype(BF16)


def token_layout(lengths, total_rows):
    ends_at = jnp.cumsum(lengths)
    starts_at = ends_at - lengths
    indices = jnp.arange(total_rows, dtype=jnp.int32)
    begins = jnp.max(
        jnp.where(starts_at[None, :] <= indices[:, None], starts_at[None, :], 0), axis=1
    )
    return ((PLEN + indices - begins).astype(F32), begins)


def rope_tables(positions):
    halves = HD // 2
    steps_float = jnp.arange(halves, dtype=F32)
    inverse = jnp.exp(steps_float * (-2.0 * math.log(10000.0) / HD))
    angles = positions[:, None] * inverse[None, :]
    return (jnp.cos(angles), jnp.sin(angles))


def route_tables(group_prefix, chips):
    slots = jnp.arange(2 * chips, dtype=jnp.int32)
    chip = jnp.arange(chips, dtype=jnp.int32)
    wanted = group_prefix[None, :] == slots[:, None]
    group_chip = slots // 2
    beyond = group_chip[None, None, :] > chip[:, None, None]
    before = group_chip[None, None, :] < chip[:, None, None]
    right = jnp.any(wanted[None] & beyond, axis=2) & (group_chip[None, :] <= chip[:, None])
    left = jnp.any(wanted[None] & before, axis=2) & (group_chip[None, :] >= chip[:, None])
    earlier = slots[None, :] < slots[:, None]

    def ranks(need):
        return jnp.sum((need[:, None, :] & earlier[None]).astype(jnp.int32), axis=2)

    most = jnp.maximum(
        jnp.max(jnp.sum(right.astype(jnp.int32), axis=1)),
        jnp.max(jnp.sum(left.astype(jnp.int32), axis=1)),
    )
    return right, ranks(right), left, ranks(left), most


def route_choice(group_prefix, tables, group, chips, width):
    right, right_rank, left, left_rank, _ = tables
    chip, core = group // 2, group % 2
    slots = jnp.arange(2 * chips, dtype=jnp.int32)
    own = slots // 2 == chip
    from_left = 2 + right_rank[jnp.maximum(chip - 1, 0)]
    from_right = 2 + left_rank[jnp.minimum(chip + 1, chips - 1)]
    held_right = jnp.where(own, slots % 2, from_left)
    held_left = jnp.where(own, slots % 2, from_right)
    final = jnp.where(
        own, slots % 2, jnp.where(slots < 2 * chip, from_left, 2 * width + from_right)
    )
    wanted = slots == group_prefix[group]
    choices = [jnp.sum(jnp.where(wanted, final, 0))]
    places = jnp.arange(width, dtype=jnp.int32) * 2 + core
    for need, rank, held in (
        (right[chip], right_rank[chip], held_right),
        (left[chip], left_rank[chip], held_left),
    ):
        hit = need[None, :] & (rank[None, :] == places[:, None])
        choices.append(jnp.sum(jnp.where(hit, held[None, :], 0), axis=1))
    return jnp.concatenate([choices[0][None], choices[1], choices[2]]).astype(jnp.int32)


def pick(number, candidates):
    result = candidates[0]
    for i in range(1, len(candidates)):
        result = jnp.where(number == i, candidates[i], result)
    return result


def gather_kernel(
    parts, chips, width, sub,
    choice, tokens, prefix, segment, kv_out,
    packed, own, held_l, held_r, stage_r, stage_l, ag,
    ag_send, ag_recv, a2a_send, a2a_recv, own_send, own_recv,
    r_send, r_recv, l_send, l_recv, rf_send, rf_recv, lf_send, lf_recv,
):
    me = lax.axis_index("tensor")
    group = lax.axis_index("dp")
    chip, core = group // 2, group % 2
    other = 1 - core
    sibling = chip * 2 + other
    groups = 2 * chips
    chunks = parts * sub
    chunk_rows = prefix.shape[0] // sub

    barrier = pltpu.get_barrier_semaphore()
    for d in range(1, parts):
        pl.semaphore_signal(
            barrier, inc=1, device_id={"tensor": lax.rem(me + d, parts)}, device_id_type=MESH
        )
    near = (sibling, lax.rem(group + 2, groups), lax.rem(group + groups - 2, groups))
    for to in near:
        pl.semaphore_signal(barrier, inc=1, device_id={"dp": to}, device_id_type=MESH)

    rows_i = lax.broadcasted_iota(jnp.int32, (2 * KVH * HD, LANES), 0)
    cols_i = lax.broadcasted_iota(jnp.int32, (2 * KVH * HD, LANES), 1)
    source = cols_i + jnp.where(cols_i >= HD, KVH * HD - HD, 0)
    for h in range(KVH):
        take = (rows_i == source + h * HD).astype(F32).astype(BF16)
        packed[h] = (
            jnp.dot(prefix[...], take, preferred_element_type=F32)
            .astype(BF16)
            .reshape(sub, chunk_rows, LANES)
        )
    pl.semaphore_wait(barrier, parts - 1 + 3)

    copies = []
    for d in range(parts - 1, 0, -1):
        to = lax.rem(me + d, parts)
        copy = pltpu.make_async_remote_copy(
            src_ref=packed.at[to * KVH // parts],
            dst_ref=own.at[core, pl.ds((parts - d) * sub, sub)],
            send_sem=a2a_send.at[parts - d],
            recv_sem=a2a_recv.at[parts - d],
            device_id={"tensor": to},
            device_id_type=MESH,
        )
        copy.start()
        copies.append(copy)
    own[core, 0:sub] = packed[me * KVH // parts]

    ag[0] = norm_rows(tokens[...])
    ag_copies = []
    for d in range(1, parts):
        copy = pltpu.make_async_remote_copy(
            src_ref=ag.at[0],
            dst_ref=ag.at[d],
            send_sem=ag_send.at[d],
            recv_sem=ag_recv.at[d],
            device_id={"tensor": lax.rem(me + d, parts)},
            device_id_type=MESH,
        )
        copy.start()
        ag_copies.append(copy)

    def lane_copy(src, dst, send_sem, recv_sem, to):
        return pltpu.make_async_remote_copy(
            src_ref=src, dst_ref=dst, send_sem=send_sem, recv_sem=recv_sem,
            device_id={"dp": to}, device_id_type=MESH,
        )

    def own_copy(m):
        block = own.at[core, pl.ds(m * sub, sub)]
        return lane_copy(block, block, own_send.at[m], own_recv.at[m], sibling)

    def flow(k, has_from, has_to, to, base, held, stage, send, recv, f_send, f_recv):
        def hop(w):
            return lane_copy(
                stage.at[w, k], held.at[w * 2 + core, k], send.at[w, k], recv.at[w, k], to
            )

        def forward(w):
            ref = held.at[w * 2 + core, k]
            return lane_copy(ref, ref, f_send.at[w, k], f_recv.at[w, k], sibling)

        @pl.when(has_from)
        def _():
            for w in range(width):
                hop(w).wait_recv()
                forward(w).start()
            for w in range(width):
                forward(w).wait_recv()

        @pl.when(has_to)
        def _():
            for w in range(width):
                stage[w, k] = pick(
                    choice[base + w],
                    [own[0, k], own[1, k]] + [held[i, k] for i in range(2 * width)],
                )
                hop(w).start()

    last = chips - 1

    def step(s, carry):
        m = s // sub

        @pl.when((m < parts) & (s % sub == 0))
        def _():
            @pl.when(m > 0)
            def _():
                pltpu.make_async_remote_copy(
                    src_ref=packed.at[0],
                    dst_ref=own.at[core, pl.ds(m * sub, sub)],
                    send_sem=a2a_send.at[m],
                    recv_sem=a2a_recv.at[m],
                    device_id={"tensor": lax.rem(me + 1, parts)},
                    device_id_type=MESH,
                ).wait_recv()

            own_copy(m).start()
            own_copy(m).wait_recv()

        k = s - chip

        @pl.when((k >= 0) & (k < chunks))
        def _():
            flow(
                k, chip > 0, chip < last, lax.rem(group + 2, groups), 1,
                held_l, stage_r, r_send, r_recv, rf_send, rf_recv,
            )

        j = s - (last - chip)

        @pl.when((j >= 0) & (j < chunks))
        def _():
            flow(
                j, chip < last, chip > 0, lax.rem(group + groups - 2, groups), 1 + width,
                held_r, stage_l, l_send, l_recv, lf_send, lf_recv,
            )

        return carry

    for edge in ((chip == 0, held_l), (chip == last, held_r)):
        def clear(ref=edge[1]):
            ref[...] = jnp.zeros_like(ref)
        pl.when(edge[0])(clear)

    lax.fori_loop(0, chunks + last, step, 0)

    def finish(k, carry):
        kv_out[k] = pick(
            choice[0],
            [own[0, k], own[1, k]]
            + [held_l[i, k] for i in range(2 * width)]
            + [held_r[i, k] for i in range(2 * width)],
        )
        return carry

    lax.fori_loop(0, chunks, finish, 0)

    def drain(k, carry):
        def one(sem, has):
            @pl.when(has)
            def _():
                for w in range(width):
                    lane_copy(
                        stage_r.at[w, k], stage_r.at[w, k], sem.at[w, k], sem.at[w, k], sibling
                    ).wait_send()

        one(r_send, chip < last)
        one(l_send, chip > 0)
        one(rf_send, chip > 0)
        one(lf_send, chip < last)
        return carry

    lax.fori_loop(0, chunks, drain, 0)
    for m in range(parts):
        own_copy(m).wait_send()
    for copy in copies:
        copy.wait_send()
    segment[pl.ds(me, 1)] = ag[0:1]
    for d in range(1, parts):
        ag_copies[d - 1].wait_recv()
        segment[pl.ds(lax.rem(me + parts - d, parts), 1)] = ag[d : d + 1]
    for copy in ag_copies:
        copy.wait_send()


def gather(choice, tokens, prefix, parts, chips, width, identity):
    rows, model = tokens.shape
    shard = prefix.shape[0]
    sub = 2 if shard >= 512 else 1
    chunks = parts * sub
    piece = (chunks, shard // sub, LANES)
    dma = pltpu.SemaphoreType.DMA
    lane = [dma((width, chunks))] * 8
    segment, kv = pl.pallas_call(
        functools.partial(gather_kernel, parts, chips, width, sub),
        out_shape=(
            jax.ShapeDtypeStruct((parts, rows, model), BF16),
            jax.ShapeDtypeStruct(piece, BF16),
        ),
        in_specs=[SMEM, VMEM, VMEM],
        out_specs=(VMEM, VMEM),
        scratch_shapes=[
            pltpu.VMEM((KVH, sub, shard // sub, LANES), BF16),
            pltpu.VMEM((2,) + piece, BF16),
            pltpu.VMEM((2 * width,) + piece, BF16),
            pltpu.VMEM((2 * width,) + piece, BF16),
            pltpu.VMEM((width,) + piece, BF16),
            pltpu.VMEM((width,) + piece, BF16),
            pltpu.VMEM((parts, rows, model), BF16),
        ]
        + [dma((parts,))] * 6
        + lane,
        compiler_params=pltpu.CompilerParams(
            collective_id=identity, has_side_effects=True, vmem_limit_bytes=52 * MIB
        ),
        name="gather",
    )(choice, tokens, prefix)
    return segment.reshape(parts * rows, model), kv.reshape(PLEN, LANES)


def attention_kernel(heads, x_ref, wq_ref, wkv_ref, cos_ref, sin_ref, begin_ref, kv_ref,
                     out_ref, queries, keys, values, scores):
    rows = x_ref.shape[0]
    lane = lax.broadcasted_iota(jnp.int32, (1, LANES), 1)
    former = (lane % HD) < HD // 2
    low = lane < HD

    def rotated(tile, cos_table, sin_table):
        swapped = jnp.where(
            former, -pltpu.roll(tile, LANES - HD // 2, 1), pltpu.roll(tile, HD // 2, 1)
        )
        return tile * cos_table + swapped * sin_table

    x = x_ref[...]
    mapped = jnp.dot(x, wq_ref[...], preferred_element_type=F32)
    cos_table, sin_table = cos_ref[...], sin_ref[...]
    for h in range(heads):
        if h % 2 == 0:
            tile = mapped[:, (h // 2) * LANES : (h // 2 + 1) * LANES]
            tile = rotated(tile, cos_table, sin_table).astype(BF16).astype(F32) * 0.125
            head = tile
        else:
            head = pltpu.roll(tile, HD, 1)
        queries[h] = jnp.where(low, head, 0.0).astype(BF16)
    pair = jnp.dot(x, wkv_ref[...], preferred_element_type=F32)
    pair = jnp.where(low, rotated(pair, cos_table, sin_table), pair)
    keys[0:PLEN, :] = kv_ref[...]
    keys[PLEN:, :] = pair.astype(BF16)
    values[...] = jnp.where(low, 1.0, keys[...].astype(F32)).astype(BF16)

    block = 256 if rows % 256 == 0 else rows
    step = 512
    total = PLEN + rows
    per_head = rows // block

    def one(i, carry):
        h, b = i // per_head, i % per_head
        start = pl.multiple_of(b * block, block)
        query = queries[h, pl.ds(start, block), :]
        top = jnp.full((block, LANES), NEG_FILL, F32)
        for n in range(total // step):
            part = lax.dot_general(
                query, keys[n * step : (n + 1) * step, :], (((1,), (1,)), ((), ())),
                preferred_element_type=F32,
            )
            if n * step >= PLEN:
                place = lax.broadcasted_iota(jnp.int32, (block, step), 1) + (n * step - PLEN)
                row = lax.broadcasted_iota(jnp.int32, (block, step), 0) + start
                seen = (place >= begin_ref[pl.ds(start, block), 0:1]) & (place <= row)
                part = jnp.where(seen, part, NEG_FILL)
            scores[:, n * step : (n + 1) * step] = part
            for q in range(step // LANES):
                top = jnp.maximum(top, part[:, q * LANES : (q + 1) * LANES])
        top = jnp.max(top, axis=1, keepdims=True)
        blended = jnp.zeros((block, LANES), F32)
        for n in range(total // step):
            weight = jnp.exp(scores[:, n * step : (n + 1) * step] - top).astype(BF16)
            blended += jnp.dot(
                weight, values[n * step : (n + 1) * step, :], preferred_element_type=F32
            )
        result = jnp.where(low, 0.0, blended / pltpu.roll(blended, HD, 1))
        out_ref[h, pl.ds(start, block), :] = result.astype(BF16)
        return carry

    lax.fori_loop(0, heads * per_head, one, 0)


def attention(x, wq, wkv, cos_table, sin_table, begins, kv, heads):
    rows = x.shape[0]
    total = PLEN + rows
    block = 256 if rows % 256 == 0 else rows
    out = pl.pallas_call(
        functools.partial(attention_kernel, heads),
        out_shape=jax.ShapeDtypeStruct((heads, rows, LANES), BF16),
        in_specs=[VMEM] * 7,
        out_specs=VMEM,
        scratch_shapes=[
            pltpu.VMEM((heads, rows, LANES), BF16),
            pltpu.VMEM((total, LANES), BF16),
            pltpu.VMEM((total, LANES), BF16),
            pltpu.VMEM((block, total), F32),
        ],
        compiler_params=pltpu.CompilerParams(vmem_limit_bytes=52 * MIB),
        name="attention",
    )(x, wq, wkv, cos_table, sin_table, begins, kv)
    return out


def mlp_kernel(
    parts, att, out_w, tokens, gate_up, down, result,
    gu_v, dn_v, a_send, a_recv, rows_v, f_send, f_recv, hidden,
    w_sem, as_sem, ar_sem, gs_sem, gr_sem, fs_sem, fr_sem,
):
    me = lax.axis_index("tensor")
    rows = tokens.shape[0]
    model = tokens.shape[1]
    units = hidden.shape[1]
    heads = att.shape[0]
    loads = [
        pltpu.make_async_copy(gate_up, gu_v, w_sem.at[0]),
        pltpu.make_async_copy(down, dn_v, w_sem.at[1]),
    ]
    for load in loads:
        load.start()
    barrier = pltpu.get_barrier_semaphore()
    for d in range(1, parts):
        pl.semaphore_signal(
            barrier, inc=1, device_id={"tensor": lax.rem(me + d, parts)}, device_id_type=MESH
        )

    def send(src, dst, send_sem, recv_sem, to):
        return pltpu.make_async_remote_copy(
            src_ref=src, dst_ref=dst, send_sem=send_sem, recv_sem=recv_sem,
            device_id={"tensor": to}, device_id_type=MESH,
        )

    def partial_out(owner):
        start = pl.multiple_of(owner * rows, rows)
        total = jnp.zeros((rows, model), F32)
        for h in range(heads):
            total += jnp.dot(
                att[h, pl.ds(start, rows), :], out_w[h], preferred_element_type=F32
            )
        return total.astype(BF16)

    copies = []
    for d in range(1, parts):
        to = lax.rem(me + d, parts)
        a_send[d] = partial_out(to)
        if d == 1:
            pl.semaphore_wait(barrier, parts - 1)
        copy = send(a_send.at[d], a_recv.at[d], as_sem.at[d], ar_sem.at[d], to)
        copy.start()
        copies.append(copy)
    total = partial_out(me).astype(F32)
    for d in range(1, parts):
        copies[d - 1].wait_recv()
        total += a_recv[d].astype(F32)
    middle = (tokens[...].astype(F32) + total).astype(BF16)
    a_send[0] = middle
    rows_v[0] = norm_rows(middle)
    sends = []
    for d in range(1, parts):
        copy = send(
            rows_v.at[0], rows_v.at[d], gs_sem.at[d], gr_sem.at[d], lax.rem(me + d, parts)
        )
        copy.start()
        sends.append(copy)
    for load in loads:
        load.wait()

    tile = 256 if units % 256 == 0 else units
    out_tile = 512
    backs = []
    for d in range(parts):
        if d > 0:
            sends[d - 1].wait_recv()

        def up(i, carry, d=d):
            if tile == units:
                at = slice(None)
            else:
                at = pl.ds(pl.multiple_of(i * tile, tile), tile)
            x = rows_v[d]
            gate = jnp.dot(x, gu_v[0, :, at], preferred_element_type=F32)
            raised = jnp.dot(x, gu_v[1, :, at], preferred_element_type=F32)
            hidden[:, at] = (gate / (1.0 + jnp.exp(-gate)) * raised).astype(BF16)
            return carry

        lax.fori_loop(0, units // tile, up, 0)

        def lower(i, carry, d=d):
            at = pl.ds(pl.multiple_of(i * out_tile, out_tile), out_tile)
            f_send[d, :, at] = jnp.dot(
                hidden[...], dn_v[:, at], preferred_element_type=F32
            ).astype(BF16)
            return carry

        lax.fori_loop(0, model // out_tile, lower, 0)
        if d > 0:
            owner = lax.rem(me + parts - d, parts)
            copy = send(f_send.at[d], f_recv.at[d], fs_sem.at[d], fr_sem.at[d], owner)
            copy.start()
            backs.append(copy)
    total = f_send[0].astype(F32)
    for d in range(1, parts):
        backs[d - 1].wait_recv()
        total += f_recv[d].astype(F32)
    result[...] = (a_send[0].astype(F32) + total).astype(BF16)
    for copy in copies + sends + backs:
        copy.wait_send()


def mlp(att, out_w, tokens, gate_up, down, parts, identity):
    rows, model = tokens.shape
    dma = pltpu.SemaphoreType.DMA
    full = pltpu.VMEM((parts, rows, model), BF16)
    return pl.pallas_call(
        functools.partial(mlp_kernel, parts),
        out_shape=jax.ShapeDtypeStruct((rows, model), BF16),
        in_specs=[VMEM, VMEM, VMEM, ANY, ANY],
        out_specs=VMEM,
        scratch_shapes=[
            pltpu.VMEM(gate_up.shape, BF16),
            pltpu.VMEM(down.shape, BF16),
            full, full, full, full, full,
            pltpu.VMEM((rows, down.shape[0]), BF16),
            dma((2,)),
        ]
        + [dma((parts,))] * 6,
        compiler_params=pltpu.CompilerParams(
            collective_id=identity, has_side_effects=True, vmem_limit_bytes=52 * MIB
        ),
        name="mlp",
    )(att, out_w, tokens, gate_up, down)


def on_device(
    tokens,
    lengths,
    group_prefix,
    prefix_cache,
    query_weight,
    key_weight,
    value_weight,
    out_weight,
    gate_up_weight,
    down_weight,
):
    parts = lax.axis_size("tensor")
    chips = lax.axis_size("dp") // 2
    rank = lax.axis_index("tensor")
    group = lax.axis_index("dp")
    rows = tokens.shape[0] * parts
    heads = query_weight.shape[1] // HD
    kv_head = rank * heads // (QH // KVH)

    tables = route_tables(group_prefix, chips)
    most = tables[-1]

    def routed(width, identity):
        def run(prefix, rows_in):
            choice = route_choice(group_prefix, tables, group, chips, width)
            return gather(choice, rows_in, prefix, parts, chips, width, identity)
        return run

    segment, kv = lax.cond(
        most <= 2, routed(1, 0), routed(chips // 2, 1), prefix_cache, tokens
    )

    positions, begins = token_layout(lengths[0], rows)
    cos_half, sin_half = rope_tables(positions)
    cos_table = jnp.concatenate([cos_half] * 4, axis=1)
    sin_table = jnp.concatenate([sin_half] * 4, axis=1)
    wkv = jnp.concatenate(
        [
            lax.dynamic_slice_in_dim(key_weight, kv_head * HD, HD, 1),
            lax.dynamic_slice_in_dim(value_weight, kv_head * HD, HD, 1),
        ],
        axis=1,
    )
    wq = query_weight
    if heads % 2:
        wq = jnp.pad(wq, ((0, 0), (0, HD)))
    att = attention(
        segment, wq, wkv, cos_table, sin_table, begins[:, None], kv, heads
    )
    out_w = jnp.pad(
        out_weight.reshape(heads, HD, out_weight.shape[1]), ((0, 0), (HD, 0), (0, 0))
    )
    return mlp(att, out_w, tokens, gate_up_weight, down_weight, parts, 2)


def solution(mesh):
    return jax.shard_map(
        on_device,
        mesh=mesh,
        in_specs=(
            P(("dp", "tensor"), None),
            P("dp", None),
            P(),
            P(("dp", "tensor"), None),
            P(None, "tensor"),
            P(),
            P(),
            P("tensor", None),
            P(None, None, "tensor"),
            P("tensor", None),
        ),
        out_specs=P(("dp", "tensor"), None),
        check_vma=False,
    )
```

time: 390 us -> 184 us (0.47)
  waiting for transfers between devices: 228 us -> 0 us
  Pallas kernels: 0 us -> 169 us
  other arithmetic: 80.3 us -> 8.66 us
  matrix products: 56.1 us -> 0 us
  between operations: 13.7 us -> 1.48 us
  local copies, waits for them, and re-layouts: 11.3 us -> 5.2 us
    pallas_call x0 -> x3, Pallas kernels: none -> 169 us  [the longest x1 82.3 us: mlp(): pl.pallas_call(functools.partial(mlp_kernel, parts), out_shape=jax.ShapeD...]
    all_gather x4 -> x0, waiting for transfers between devices: 156 us -> none  [the longest x1 81.1 us: on_device(): segment = lax.all_gather(prefix_cache, 'dp', axis=0, tiled=True)]
    reduce_scatter x2 -> x0, waiting for transfers between devices: 70.7 us -> none  [the longest x1 35.4 us: on_device(): lax.psum_scatter(jnp.dot(hidden, down_weight, preferred_element_type=jnp....]
    dot_general x8 -> x0, matrix products: 56.1 us -> none  [the longest x2 15.2 us: softmax_block(): jnp.einsum('thd,nhd->thn', queries, keys_block, preferred_element_type=jn...]
    scatter-add x1 -> x0, other arithmetic: 54.9 us -> none  [on_device(): chosen = jnp.zeros_like(prefix_cache).at[places].add(jnp.where(matches[:,...]
    reduce_sum x5 -> x4, other arithmetic: 17.3 us -> 2.32 us  [the longest x1 1.27 us: route_choice(): choices = [jnp.sum(jnp.where(wanted, final, 0))]]
    convert_element_type x4 -> x1, other arithmetic: 6.08 us -> 0.01 us  [token_layout(): return ((PLEN + indices - begins).astype(F32), begins)]
    dynamic_slice x5 -> x2, local copies, waits for them, and re-layouts: 7.9 us -> 2.64 us  [the longest x1 1.4 us: on_device(): lax.dynamic_slice_in_dim(value_weight, kv_head * HD, HD, 1)]
  transfers between devices with their start and end apart: 6 -> 0, of which waited for: 5 -> 0; matrix products, arithmetic and copies ran while one was open for 18% -> 0% of each run, Pallas kernels for 0% -> 0%
where the time goes in v1:
time: 184 us
  Pallas kernels  169 us (92%)
  other arithmetic  8.66 us (5%)
  local copies, waits for them, and re-layouts  5.2 us (3%)
    pallas_call x1, Pallas kernels, mlp(): pl.pallas_call(functools.partial(mlp_kernel, parts), out_shape=jax.ShapeD...  82.3 us
    pallas_call x1, Pallas kernels, gather(): pl.pallas_call(functools.partial(gather_kernel, parts, chips, width, sub)...  67.9 us
    pallas_call x1, Pallas kernels, attention(): pl.pallas_call(functools.partial(attention_kernel, heads), out_shape=jax....  18.3 us

profile of v1, /device:TPU:0, one launch (start us, length us, event | category | flops | bytes accessed | tf_op | source)
XLA Modules:
  0.0 184.1 jit_solution(325669081404265335)
XLA Ops:
  0.0 0.0 copy-start.2
  0.0 0.7 iota_compare_fusion.2
  0.8 0.2 and_reduce_fusion
  1.0 0.2 convert_reduce_fusion.2
  1.2 0.2 convert_reduce_fusion
  1.4 0.6 reduce_max.29
  2.0 0.7 reduce_max.30
  4.1 73.3 %conditional.1 = (bf16[512,2048]{1,0:T(8,128)(2,1)S(1)}, bf16[4096,128]{1,0:T(8,128)(2,1)}) conditional(s32[]{:T(128)} %convert_element_type.26, (s32[]{:T(128)}, s32[8]{0:T(128)}, s32[4,8]{1,0:T(4,128)S(1)}, s32[4,8]{1,0:T(4,128)S(1)}, pred[4,8]{1,0:T(4,128)(4,1)S(1)}, /*index=5*/pred[4,8]{1,0:T(4,128)(4,1)S(1)}, bf16[128,2048]{1,0:T(8,128)(2,1)}, ...), branch_computations={%region_8.12_spmd, %region_12.16_spmd} | conditional | flops 473 | bytes 984 | solution.py:573
  4.1 1.2 dynamic_slice.39
  5.4 1.3 fusion.9
  6.6 0.7 fusion.10
  7.3 2.0 %pad_add_fusion.1.choice = s32[3]{0:T(128)S(1)} fusion(s32[1]{0:T(128)} %bitcast.17, s32[1]{0:T(128)} %bitcast.16, s32[1]{0:T(128)} %bitcast.15), kind=kLoop, calls=%fused_computation.55 | loop fusion | flops 6 | bytes 24 | tf_op jit(solution)/shard_map/cond/branch_1_fun/concatenate | solution.py:92
  9.3 67.9 %gather.3 = (bf16[4,128,2048]{2,1,0:T(8,128)(2,1)S(1)}, bf16[8,512,128]{2,1,0:T(8,128)(2,1)}) custom-call(s32[3]{0:T(128)S(1)} %pad_add_fusion.1.choice, bf16[128,2048]{1,0:T(8,128)(2,1)} %get-tuple-element.53.tokens, bf16[1024,512]{1,0:T(8,128)(2,1)} %get-tuple-element.54.prefix), custom_call_target="tpu_custom_call" | custom-call | tf_op jit(solution)/shard_map/cond/branch_1_fun/gather/pallas_call | solution.py:300
  77.4 0.0 copy-start.3
  77.4 0.0 copy-done.2
  77.4 1.4 constant_dynamic-slice_fusion.8
  78.8 0.3 pad_maximum_fusion.wkv_ref
  79.1 0.0 copy-done.3
  79.1 0.2 reduce-window_clone.1
  79.3 0.1 select_reduce_fusion
  79.4 1.0 multiply_sine_fusion
  80.4 0.5 pad_maximum_fusion.1
  80.9 0.1 copy.12.begin_ref
  81.1 0.0 copy-start.1
  81.1 18.3 %attention.1.att = bf16[4,512,128]{2,1,0:T(8,128)(2,1)S(1)} custom-call(bf16[512,2048]{1,0:T(8,128)(2,1)S(1)} %get-tuple-element.59.x_ref, bf16[2048,256]{1,0:T(8,128)(2,1)} %wq_ref.1, bf16[2048,128]{1,0:T(8,128)(2,1)S(1)} %pad_maximum_fusion.wkv_ref, f32[512,128]{1,0:T(8,128)S(1)} %get-tuple-element.89.cos_ref, f32[512,128]{1,0:T(8,128)S(1)} %get-tuple-element.90.sin_ref, ...), custom_call_target="tpu_custom_call" | custom-call | tf_op jit(solution)/shard_map/attention/pallas_call | solution.py:398
  99.3 0.0 copy-start
  99.3 0.0 copy-done.1
  99.4 1.6 pad.4.out_w
  101.0 0.0 copy-done
  101.0 82.3 %mlp.1 = bf16[128,2048]{1,0:T(8,128)(2,1)S(1)} custom-call(bf16[4,512,128]{2,1,0:T(8,128)(2,1)S(1)} %attention.1.att, bf16[4,128,2048]{2,1,0:T(8,128)(2,1)} %pad.4.out_w, bf16[128,2048]{1,0:T(8,128)(2,1)S(1)} %copy-done, bf16[2,2048,1280]{2,1,0:T(8,128)(2,1)} %gate_up.1, bf16[1280,2048]{1,0:T(8,128)(2,1)} %down.1), custom_call_target="tpu_custom_call" | custom-call | tf_op jit(solution)/shard_map/mlp/pallas_call | solution.py:524
  183.3 0.8 copy.18
  (6 shorter events, 0.0 us)
Async XLA Ops:
  0.0 77.4 %copy-start.2 = (bf16[2048,256]{1,0:T(8,128)(2,1)S(1)}, bf16[2048,256]{1,0:T(8,128)(2,1)}, u32[]{:S(2)}) copy-start(bf16[2048,256]{1,0:T(8,128)(2,1)} %param.18) | copy-start | bytes 3145732
  77.4 1.7 copy-start.3
  81.1 18.3 %copy-start.1 = (bf16[256,2048]{1,0:T(8,128)(2,1)S(1)}, bf16[256,2048]{1,0:T(8,128)(2,1)}, u32[]{:S(2)}) copy-start(bf16[256,2048]{1,0:T(8,128)(2,1)} %param.19) | copy-start | bytes 3145732
  99.3 1.6 copy-start

commit v2 on v1

--- a/solution.py
+++ b/solution.py
@@ -47,49 +47,70 @@
     return (jnp.cos(angles), jnp.sin(angles))
 
 
-def route_tables(group_prefix, chips):
+def most_crossing(group_prefix, chips):
     slots = jnp.arange(2 * chips, dtype=jnp.int32)
-    chip = jnp.arange(chips, dtype=jnp.int32)
     wanted = group_prefix[None, :] == slots[:, None]
-    group_chip = slots // 2
-    beyond = group_chip[None, None, :] > chip[:, None, None]
-    before = group_chip[None, None, :] < chip[:, None, None]
-    right = jnp.any(wanted[None] & beyond, axis=2) & (group_chip[None, :] <= chip[:, None])
-    left = jnp.any(wanted[None] & before, axis=2) & (group_chip[None, :] >= chip[:, None])
-    earlier = slots[None, :] < slots[:, None]
-
-    def ranks(need):
-        return jnp.sum((need[:, None, :] & earlier[None]).astype(jnp.int32), axis=2)
-
-    most = jnp.maximum(
-        jnp.max(jnp.sum(right.astype(jnp.int32), axis=1)),
-        jnp.max(jnp.sum(left.astype(jnp.int32), axis=1)),
-    )
-    return right, ranks(right), left, ranks(left), most
-
-
-def route_choice(group_prefix, tables, group, chips, width):
-    right, right_rank, left, left_rank, _ = tables
+    final = jnp.max(jnp.where(wanted, slots[None, :], -1), axis=1)
+    first = jnp.min(jnp.where(wanted, slots[None, :], 2 * chips), axis=1)
+    edge = 2 * jnp.arange(1, chips, dtype=jnp.int32)[:, None]
+    right = (slots[None, :] < edge) & (final[None, :] >= edge)
+    left = (slots[None, :] >= edge) & (first[None, :] < edge)
+    counts = jnp.sum(jnp.stack([right, left]).astype(jnp.int32), axis=2)
+    return jnp.max(counts)
+
+
+def route_choice(slot_ref, group, chips, width):
+    number = 2 * chips
     chip, core = group // 2, group % 2
-    slots = jnp.arange(2 * chips, dtype=jnp.int32)
-    own = slots // 2 == chip
-    from_left = 2 + right_rank[jnp.maximum(chip - 1, 0)]
-    from_right = 2 + left_rank[jnp.minimum(chip + 1, chips - 1)]
-    held_right = jnp.where(own, slots % 2, from_left)
-    held_left = jnp.where(own, slots % 2, from_right)
-    final = jnp.where(
-        own, slots % 2, jnp.where(slots < 2 * chip, from_left, 2 * width + from_right)
-    )
-    wanted = slots == group_prefix[group]
-    choices = [jnp.sum(jnp.where(wanted, final, 0))]
-    places = jnp.arange(width, dtype=jnp.int32) * 2 + core
-    for need, rank, held in (
-        (right[chip], right_rank[chip], held_right),
-        (left[chip], left_rank[chip], held_left),
-    ):
-        hit = need[None, :] & (rank[None, :] == places[:, None])
-        choices.append(jnp.sum(jnp.where(hit, held[None, :], 0), axis=1))
-    return jnp.concatenate([choices[0][None], choices[1], choices[2]]).astype(jnp.int32)
+    held = [slot_ref[g] for g in range(number)]
+    final, first = [], []
+    for s in range(number):
+        top, low = jnp.int32(-1), jnp.int32(number)
+        for g in range(number):
+            top = jnp.where(held[g] == s, g, top)
+        for g in reversed(range(number)):
+            low = jnp.where(held[g] == s, g, low)
+        final.append(top)
+        first.append(low)
+
+    def ranks(needs):
+        result, count = [], jnp.int32(0)
+        for need in needs:
+            result.append(count)
+            count = count + need.astype(jnp.int32)
+        return result
+
+    def right(z):
+        return [(s // 2 <= z) & (final[s] >= 2 * (z + 1)) for s in range(number)]
+
+    def left(z):
+        return [(s // 2 >= z) & (first[s] < 2 * z) for s in range(number)]
+
+    from_left, from_right = ranks(right(chip - 1)), ranks(left(chip + 1))
+    mine = slot_ref[group]
+    keep = jnp.int32(0)
+    sides = []
+    for s in range(number):
+        own = chip == s // 2
+        value = jnp.where(
+            own, s % 2, jnp.where(chip > s // 2, 2 + from_left[s], 2 + 2 * width + from_right[s])
+        )
+        keep = jnp.where(mine == s, value, keep)
+    for needs, source in ((right(chip), from_left), (left(chip), from_right)):
+        rank = ranks(needs)
+        chosen = []
+        for w in range(width):
+            place = 2 * w + core
+            value = jnp.int32(0)
+            for s in range(number):
+                value = jnp.where(
+                    needs[s] & (rank[s] == place),
+                    jnp.where(chip == s // 2, s % 2, 2 + source[s]),
+                    value,
+                )
+            chosen.append(value)
+        sides.append(chosen)
+    return [keep] + sides[0] + sides[1]
 
 
 def pick(number, candidates):
@@ -101,7 +122,7 @@
 
 def gather_kernel(
     parts, chips, width, sub,
-    choice, tokens, prefix, segment, kv_out,
+    slot_ref, tokens, prefix, segment, kv_out,
     packed, own, held_l, held_r, stage_r, stage_l, ag,
     ag_send, ag_recv, a2a_send, a2a_recv, own_send, own_recv,
     r_send, r_recv, l_send, l_recv, rf_send, rf_recv, lf_send, lf_recv,
@@ -124,6 +145,7 @@
     for to in near:
         pl.semaphore_signal(barrier, inc=1, device_id={"dp": to}, device_id_type=MESH)
 
+    choice = route_choice(slot_ref, group, chips, width)
     rows_i = lax.broadcasted_iota(jnp.int32, (2 * KVH * HD, LANES), 0)
     cols_i = lax.broadcasted_iota(jnp.int32, (2 * KVH * HD, LANES), 1)
     source = cols_i + jnp.where(cols_i >= HD, KVH * HD - HD, 0)
@@ -152,9 +174,8 @@
     own[core, 0:sub] = packed[me * KVH // parts]
 
     ag[0] = norm_rows(tokens[...])
-    ag_copies = []
-    for d in range(1, parts):
-        copy = pltpu.make_async_remote_copy(
+    def ag_copy(d):
+        return pltpu.make_async_remote_copy(
             src_ref=ag.at[0],
             dst_ref=ag.at[d],
             send_sem=ag_send.at[d],
@@ -162,8 +183,56 @@
             device_id={"tensor": lax.rem(me + d, parts)},
             device_id_type=MESH,
         )
-        copy.start()
-        ag_copies.append(copy)
+
+    def half_copy(slot, place, half, to):
+        rows = tokens.shape[0] // 2
+        at = pl.ds(half * rows, rows)
+        return pltpu.make_async_remote_copy(
+            src_ref=ag.at[slot, at],
+            dst_ref=ag.at[place, at],
+            send_sem=ag_send.at[2 * place + half - 2],
+            recv_sem=ag_recv.at[2 * place + half - 2],
+            device_id={"tensor": to},
+            device_id_type=MESH,
+        )
+
+    near_x, near_y = me + 1 - 2 * (me % 2), lax.rem(me + 2, parts)
+
+    def ag_start():
+        if parts == 4:
+            half_copy(0, 1, 0, near_x).start()
+            half_copy(0, 2, 1, near_y).start()
+            half_copy(0, 1, 1, near_x).start()
+            half_copy(0, 2, 0, near_y).start()
+        else:
+            for d in range(1, parts):
+                ag_copy(d).start()
+
+    def ag_forward():
+        if parts == 4:
+            half_copy(0, 1, 0, near_x).wait_recv()
+            half_copy(1, 3, 0, near_y).start()
+            half_copy(0, 2, 1, near_y).wait_recv()
+            half_copy(2, 3, 1, near_x).start()
+
+    def ag_finish():
+        segment[pl.ds(me, 1)] = ag[0:1]
+        if parts == 4:
+            half_copy(0, 1, 1, near_x).wait_recv()
+            segment[pl.ds(near_x, 1)] = ag[1:2]
+            half_copy(0, 2, 0, near_y).wait_recv()
+            segment[pl.ds(near_y, 1)] = ag[2:3]
+            half_copy(1, 3, 0, near_y).wait_recv()
+            half_copy(2, 3, 1, near_x).wait_recv()
+            segment[pl.ds(parts - 1 - me, 1)] = ag[3:4]
+            for place, half in ((1, 0), (1, 1), (2, 0), (2, 1), (3, 0), (3, 1)):
+                half_copy(0, place, half, near_x).wait_send()
+        else:
+            for d in range(1, parts):
+                ag_copy(d).wait_recv()
+                segment[pl.ds(lax.rem(me + parts - d, parts), 1)] = ag[d : d + 1]
+            for d in range(1, parts):
+                ag_copy(d).wait_send()
 
     def lane_copy(src, dst, send_sem, recv_sem, to):
         return pltpu.make_async_remote_copy(
@@ -222,6 +291,7 @@
 
             own_copy(m).start()
             own_copy(m).wait_recv()
+            pl.when(m == parts - 1)(ag_start)
 
         k = s - chip
 
@@ -241,6 +311,7 @@
                 held_r, stage_l, l_send, l_recv, lf_send, lf_recv,
             )
 
+        pl.when(s == chunks + last - 2)(ag_forward)
         return carry
 
     for edge in ((chip == 0, held_l), (chip == last, held_r)):
@@ -281,15 +352,10 @@
         own_copy(m).wait_send()
     for copy in copies:
         copy.wait_send()
-    segment[pl.ds(me, 1)] = ag[0:1]
-    for d in range(1, parts):
-        ag_copies[d - 1].wait_recv()
-        segment[pl.ds(lax.rem(me + parts - d, parts), 1)] = ag[d : d + 1]
-    for copy in ag_copies:
-        copy.wait_send()
-
-
-def gather(choice, tokens, prefix, parts, chips, width, identity):
+    ag_finish()
+
+
+def gather(slots, tokens, prefix, parts, chips, width, identity):
     rows, model = tokens.shape
     shard = prefix.shape[0]
     sub = 2 if shard >= 512 else 1
@@ -314,18 +380,57 @@
             pltpu.VMEM((width,) + piece, BF16),
             pltpu.VMEM((parts, rows, model), BF16),
         ]
-        + [dma((parts,))] * 6
+        + [dma((max(parts, 6),))] * 2
+        + [dma((parts,))] * 4
         + lane,
         compiler_params=pltpu.CompilerParams(
             collective_id=identity, has_side_effects=True, vmem_limit_bytes=52 * MIB
         ),
         name="gather",
-    )(choice, tokens, prefix)
+    )(slots, tokens, prefix)
     return segment.reshape(parts * rows, model), kv.reshape(PLEN, LANES)
 
 
-def attention_kernel(heads, x_ref, wq_ref, wkv_ref, cos_ref, sin_ref, begin_ref, kv_ref,
-                     out_ref, queries, keys, values, scores):
+def attention_kernel(heads, parts, *refs):
+    (x_ref, wq_ref, wkv_ref, cos_ref, sin_ref, begin_ref, kv_ref) = refs[:7]
+    if parts == 4:
+        ow, out_ref, ow_all, queries, keys, values, scores, w_send, w_recv, s_send, s_recv = refs[7:]
+        me = lax.axis_index("tensor")
+        group = lax.axis_index("dp")
+        core = group % 2
+        sibling = group + 1 - 2 * core
+        near_x, near_y = me + 1 - 2 * (me % 2), lax.rem(me + 2, parts)
+        quarter = ow.shape[0] // 4
+
+        def piece(src, place, half, to):
+            at = pl.ds((2 * core + half) * quarter, quarter)
+            return pltpu.make_async_remote_copy(
+                src_ref=ow.at[at] if src == 0 else ow_all.at[src, at],
+                dst_ref=ow_all.at[place, at],
+                send_sem=w_send.at[2 * place + half - 2],
+                recv_sem=w_recv.at[2 * place + half - 2],
+                device_id={"tensor": to},
+                device_id_type=MESH,
+            )
+
+        def share(place):
+            ref = ow_all.at[place, pl.ds(2 * core * quarter, 2 * quarter)]
+            return pltpu.make_async_remote_copy(
+                src_ref=ref, dst_ref=ref, send_sem=s_send.at[place - 1],
+                recv_sem=s_recv.at[place - 1], device_id={"dp": sibling}, device_id_type=MESH,
+            )
+
+        barrier = pltpu.get_barrier_semaphore()
+        for to in ({"tensor": near_x}, {"tensor": near_y}, {"dp": sibling}):
+            pl.semaphore_signal(barrier, inc=1, device_id=to, device_id_type=MESH)
+        pl.semaphore_wait(barrier, 3)
+        piece(0, 1, 0, near_x).start()
+        piece(0, 2, 1, near_y).start()
+        piece(0, 1, 1, near_x).start()
+        piece(0, 2, 0, near_y).start()
+        ow_all[0] = ow[...]
+    else:
+        out_ref, queries, keys, values, scores = refs[7:]
     rows = x_ref.shape[0]
     lane = lax.broadcasted_iota(jnp.int32, (1, LANES), 1)
     former = (lane % HD) < HD // 2
@@ -358,10 +463,9 @@
     step = 512
     total = PLEN + rows
     per_head = rows // block
-
-    def one(i, carry):
-        h, b = i // per_head, i % per_head
-        start = pl.multiple_of(b * block, block)
+    pairs = (heads + 1) // 2
+
+    def one_head(h, start, slot):
         query = queries[h, pl.ds(start, block), :]
         top = jnp.full((block, LANES), NEG_FILL, F32)
         for n in range(total // step):
@@ -374,42 +478,89 @@
                 row = lax.broadcasted_iota(jnp.int32, (block, step), 0) + start
                 seen = (place >= begin_ref[pl.ds(start, block), 0:1]) & (place <= row)
                 part = jnp.where(seen, part, NEG_FILL)
-            scores[:, n * step : (n + 1) * step] = part
+            scores[slot, :, n * step : (n + 1) * step] = part
             for q in range(step // LANES):
                 top = jnp.maximum(top, part[:, q * LANES : (q + 1) * LANES])
         top = jnp.max(top, axis=1, keepdims=True)
         blended = jnp.zeros((block, LANES), F32)
         for n in range(total // step):
-            weight = jnp.exp(scores[:, n * step : (n + 1) * step] - top).astype(BF16)
+            weight = jnp.exp(scores[slot, :, n * step : (n + 1) * step] - top).astype(BF16)
             blended += jnp.dot(
                 weight, values[n * step : (n + 1) * step, :], preferred_element_type=F32
             )
-        result = jnp.where(low, 0.0, blended / pltpu.roll(blended, HD, 1))
-        out_ref[h, pl.ds(start, block), :] = result.astype(BF16)
+        return blended
+
+    def one(i, carry):
+        if parts == 4:
+            @pl.when(i == 1)
+            def _():
+                piece(0, 1, 0, near_x).wait_recv()
+                piece(1, 3, 0, near_y).start()
+                piece(0, 2, 1, near_y).wait_recv()
+                piece(2, 3, 1, near_x).start()
+
+            @pl.when(i == pairs * per_head - 1)
+            def _():
+                piece(0, 1, 1, near_x).wait_recv()
+                share(1).start()
+                piece(0, 2, 0, near_y).wait_recv()
+                share(2).start()
+
+        p, b = i // per_head, i % per_head
+        start = pl.multiple_of(b * block, block)
+        even = one_head(2 * p, start, 0)
+        even = pltpu.roll(even, HD, 1) / even
+        if heads > 1:
+            odd = one_head(2 * p + 1, start, 1)
+            odd = odd / pltpu.roll(odd, HD, 1)
+        else:
+            odd = jnp.zeros_like(even)
+        at = pl.ds(pl.multiple_of(p * LANES, LANES), LANES)
+        out_ref[pl.ds(start, block), at] = jnp.where(low, even, odd).astype(BF16)
         return carry
 
-    lax.fori_loop(0, heads * per_head, one, 0)
-
-
-def attention(x, wq, wkv, cos_table, sin_table, begins, kv, heads):
+    lax.fori_loop(0, pairs * per_head, one, 0)
+    if parts == 4:
+        piece(1, 3, 0, near_y).wait_recv()
+        piece(2, 3, 1, near_x).wait_recv()
+        share(3).start()
+        for place in (1, 2, 3):
+            share(place).wait_recv()
+        for place in (1, 2, 3):
+            share(place).wait_send()
+            for half in range(2):
+                piece(0, place, half, near_x).wait_send()
+
+
+def attention(x, wq, wkv, cos_table, sin_table, begins, kv, out_w, heads, parts, identity):
     rows = x.shape[0]
     total = PLEN + rows
     block = 256 if rows % 256 == 0 else rows
-    out = pl.pallas_call(
-        functools.partial(attention_kernel, heads),
-        out_shape=jax.ShapeDtypeStruct((heads, rows, LANES), BF16),
-        in_specs=[VMEM] * 7,
-        out_specs=VMEM,
-        scratch_shapes=[
-            pltpu.VMEM((heads, rows, LANES), BF16),
-            pltpu.VMEM((total, LANES), BF16),
-            pltpu.VMEM((total, LANES), BF16),
-            pltpu.VMEM((block, total), F32),
-        ],
-        compiler_params=pltpu.CompilerParams(vmem_limit_bytes=52 * MIB),
+    width = (heads + 1) // 2 * LANES
+    exchange = parts == 4
+    shapes = [jax.ShapeDtypeStruct((rows, width), BF16)]
+    operands = [x, wq, wkv, cos_table, sin_table, begins, kv]
+    scratch = [
+        pltpu.VMEM((heads, rows, LANES), BF16),
+        pltpu.VMEM((total, LANES), BF16),
+        pltpu.VMEM((total, LANES), BF16),
+        pltpu.VMEM((2, block, total), F32),
+    ]
+    params = dict(vmem_limit_bytes=52 * MIB)
+    if exchange:
+        operands.append(out_w)
+        shapes.append(jax.ShapeDtypeStruct((parts,) + out_w.shape, BF16))
+        scratch += [pltpu.SemaphoreType.DMA((6,))] * 2 + [pltpu.SemaphoreType.DMA((3,))] * 2
+        params.update(collective_id=identity, has_side_effects=True)
+    return pl.pallas_call(
+        functools.partial(attention_kernel, heads, parts),
+        out_shape=shapes,
+        in_specs=[VMEM] * len(operands),
+        out_specs=[VMEM] * len(shapes),
+        scratch_shapes=scratch,
+        compiler_params=pltpu.CompilerParams(**params),
         name="attention",
-    )(x, wq, wkv, cos_table, sin_table, begins, kv)
-    return out
+    )(*operands)
 
 
 def mlp_kernel(
@@ -421,7 +572,6 @@
     rows = tokens.shape[0]
     model = tokens.shape[1]
     units = hidden.shape[1]
-    heads = att.shape[0]
     loads = [
         pltpu.make_async_copy(gate_up, gu_v, w_sem.at[0]),
         pltpu.make_async_copy(down, dn_v, w_sem.at[1]),
@@ -442,12 +592,9 @@
 
     def partial_out(owner):
         start = pl.multiple_of(owner * rows, rows)
-        total = jnp.zeros((rows, model), F32)
-        for h in range(heads):
-            total += jnp.dot(
-                att[h, pl.ds(start, rows), :], out_w[h], preferred_element_type=F32
-            )
-        return total.astype(BF16)
+        return jnp.dot(
+            att[pl.ds(start, rows), :], out_w[...], preferred_element_type=F32
+        ).astype(BF16)
 
     copies = []
     for d in range(1, parts):
@@ -515,6 +662,168 @@
     result[...] = (a_send[0].astype(F32) + total).astype(BF16)
     for copy in copies + sends + backs:
         copy.wait_send()
+
+
+def mlp_square_kernel(
+    att, out_w, tokens, gate_up, down, result,
+    gu_v, dn_v, att_v, mid_v, rows_v, f_v, f_in, hidden,
+    w_sem, as_sem, ar_sem, gs_sem, gr_sem, fs_sem, fr_sem,
+):
+    parts = 4
+    me = lax.axis_index("tensor")
+    near_x, near_y, far = me + 1 - 2 * (me % 2), lax.rem(me + 2, parts), parts - 1 - me
+    rows, model = tokens.shape
+    half_rows = rows // 2
+    units = hidden.shape[1]
+    loads = [
+        pltpu.make_async_copy(gate_up, gu_v, w_sem.at[0]),
+        pltpu.make_async_copy(down, dn_v, w_sem.at[1]),
+    ]
+    for load in loads:
+        load.start()
+    barrier = pltpu.get_barrier_semaphore()
+    for to in (near_x, near_y, far):
+        pl.semaphore_signal(barrier, inc=1, device_id={"tensor": to}, device_id_type=MESH)
+    pl.semaphore_wait(barrier, parts - 1)
+
+    def send(src, dst, send_sem, recv_sem, to):
+        return pltpu.make_async_remote_copy(
+            src_ref=src, dst_ref=dst, send_sem=send_sem, recv_sem=recv_sem,
+            device_id={"tensor": to}, device_id_type=MESH,
+        )
+
+    def cut(half):
+        return pl.ds(half * half_rows, half_rows)
+
+    def block_of(owner):
+        return att.at[pl.ds(pl.multiple_of(owner * rows, rows), rows)]
+
+    swaps = [
+        send(block_of(to), att_v.at[slot], as_sem.at[slot], ar_sem.at[slot], to)
+        for slot, to in ((3, far), (1, near_x), (2, near_y))
+    ]
+    for copy in swaps:
+        copy.start()
+
+    def group_term(block, slot):
+        term = jnp.dot(block, out_w[slot], preferred_element_type=F32)
+        return term.astype(BF16).astype(F32)
+
+    total = group_term(att[pl.ds(pl.multiple_of(me * rows, rows), rows), :], 0)
+    for copy, slot in zip(swaps[1:] + swaps[:1], (1, 2, 3)):
+        copy.wait_recv()
+        total += group_term(att_v[slot], slot)
+    middle = (tokens[...].astype(F32) + total).astype(BF16)
+    mid_v[...] = middle
+    rows_v[0] = norm_rows(middle)
+
+    def piece(src, place, half, to):
+        at = 2 * place + half - 2
+        return send(
+            rows_v.at[src, cut(half)], rows_v.at[place, cut(half)],
+            gs_sem.at[at], gr_sem.at[at], to,
+        )
+
+    piece(0, 1, 0, near_x).start()
+    piece(0, 2, 1, near_y).start()
+    piece(0, 1, 1, near_x).start()
+    piece(0, 2, 0, near_y).start()
+    for load in loads:
+        load.wait()
+
+    tile = 256 if units % 256 == 0 else units
+    out_tile = 512
+
+    def feed(first, count):
+        many = count * rows
+
+        def up(i, carry):
+            at = pl.ds(pl.multiple_of(i * tile, tile), tile)
+            x = rows_v[first : first + count].reshape(many, model)
+            gate = jnp.dot(x, gu_v[0, :, at], preferred_element_type=F32)
+            raised = jnp.dot(x, gu_v[1, :, at], preferred_element_type=F32)
+            hidden[0:many, at] = (gate / (1.0 + jnp.exp(-gate)) * raised).astype(BF16)
+            return carry
+
+        lax.fori_loop(0, units // tile, up, 0)
+
+        def lower(i, carry):
+            at = pl.ds(pl.multiple_of(i * out_tile, out_tile), out_tile)
+            f_v[first : first + count, :, at] = (
+                jnp.dot(hidden[0:many, :], dn_v[:, at], preferred_element_type=F32)
+                .astype(BF16)
+                .reshape(count, rows, out_tile)
+            )
+            return carry
+
+        lax.fori_loop(0, model // out_tile, lower, 0)
+
+    def back(slot, half, place, to):
+        at = 2 * place + half
+        return send(
+            f_v.at[slot, cut(half)], f_in.at[place, cut(half)], fs_sem.at[at], fr_sem.at[at], to
+        )
+
+    feed(0, 1)
+    piece(0, 1, 0, near_x).wait_recv()
+    piece(1, 3, 0, near_y).start()
+    piece(0, 2, 1, near_y).wait_recv()
+    piece(2, 3, 1, near_x).start()
+    piece(0, 1, 1, near_x).wait_recv()
+    piece(0, 2, 0, near_y).wait_recv()
+    feed(1, 2)
+    back(1, 0, 0, near_x).start()
+    back(2, 1, 1, near_y).start()
+    piece(1, 3, 0, near_y).wait_recv()
+    piece(2, 3, 1, near_x).wait_recv()
+    feed(3, 1)
+    back(3, 0, 2, near_x).start()
+    back(3, 1, 2, near_y).start()
+    for half, slot, place, to in ((0, 2, 1, near_y), (1, 1, 0, near_x)):
+        back(3, half, 2, to).wait_recv()
+        f_v[slot, cut(half)] = (
+            f_v[slot, cut(half)].astype(F32) + f_in[2, cut(half)].astype(F32)
+        ).astype(BF16)
+        back(slot, half, place, to).start()
+    order = ((1, 0, 0, near_x), (2, 1, 1, near_y), (2, 0, 1, near_y), (1, 1, 0, near_x))
+    for slot, half, place, to in order:
+        back(slot, half, place, to).wait_recv()
+    total = f_v[0].astype(F32) + f_in[0].astype(F32) + f_in[1].astype(F32)
+    result[...] = (mid_v[...].astype(F32) + total).astype(BF16)
+    for copy in swaps:
+        copy.wait_send()
+    for place in (1, 2, 3):
+        for half in range(2):
+            piece(0, place, half, near_x).wait_send()
+            back(1, half, place - 1, near_x).wait_send()
+
+
+def mlp_square(att, out_w, tokens, gate_up, down, identity):
+    rows, model = tokens.shape
+    parts = 4
+    dma = pltpu.SemaphoreType.DMA
+    full = pltpu.VMEM((parts, rows, model), BF16)
+    return pl.pallas_call(
+        mlp_square_kernel,
+        out_shape=jax.ShapeDtypeStruct((rows, model), BF16),
+        in_specs=[VMEM, VMEM, VMEM, ANY, ANY],
+        out_specs=VMEM,
+        scratch_shapes=[
+            pltpu.VMEM(gate_up.shape, BF16),
+            pltpu.VMEM(down.shape, BF16),
+            pltpu.VMEM((parts, rows, att.shape[1]), BF16),
+            pltpu.VMEM((rows, model), BF16),
+            full, full,
+            pltpu.VMEM((3, rows, model), BF16),
+            pltpu.VMEM((2 * rows, down.shape[0]), BF16),
+            dma((2,)), dma((parts,)), dma((parts,)),
+        ]
+        + [dma((6,))] * 4,
+        compiler_params=pltpu.CompilerParams(
+            collective_id=identity, has_side_effects=True, vmem_limit_bytes=52 * MIB
+        ),
+        name="mlp",
+    )(att, out_w, tokens, gate_up, down)
 
 
 def mlp(att, out_w, tokens, gate_up, down, parts, identity):
@@ -556,18 +865,15 @@
     parts = lax.axis_size("tensor")
     chips = lax.axis_size("dp") // 2
     rank = lax.axis_index("tensor")
-    group = lax.axis_index("dp")
     rows = tokens.shape[0] * parts
     heads = query_weight.shape[1] // HD
     kv_head = rank * heads // (QH // KVH)
 
-    tables = route_tables(group_prefix, chips)
-    most = tables[-1]
+    most = most_crossing(group_prefix, chips)
 
     def routed(width, identity):
         def run(prefix, rows_in):
-            choice = route_choice(group_prefix, tables, group, chips, width)
-            return gather(choice, rows_in, prefix, parts, chips, width, identity)
+            return gather(group_prefix, rows_in, prefix, parts, chips, width, identity)
         return run
 
     segment, kv = lax.cond(
@@ -588,13 +894,15 @@
     wq = query_weight
     if heads % 2:
         wq = jnp.pad(wq, ((0, 0), (0, HD)))
-    att = attention(
-        segment, wq, wkv, cos_table, sin_table, begins[:, None], kv, heads
+    outputs = attention(
+        segment, wq, wkv, cos_table, sin_table, begins[:, None], kv, out_weight, heads, parts, 3
     )
-    out_w = jnp.pad(
-        out_weight.reshape(heads, HD, out_weight.shape[1]), ((0, 0), (HD, 0), (0, 0))
-    )
-    return mlp(att, out_w, tokens, gate_up_weight, down_weight, parts, 2)
+    if parts == 4:
+        return mlp_square(*outputs, tokens, gate_up_weight, down_weight, 2)
+    out_w = out_weight
+    if heads % 2:
+        out_w = jnp.pad(out_w, ((0, HD), (0, 0)))
+    return mlp(outputs[0], out_w, tokens, gate_up_weight, down_weight, parts, 2)
 
 
 def solution(mesh):

time: 184 us -> 148 us (0.80)
  Pallas kernels: 169 us -> 139 us
  other arithmetic: 8.66 us -> 5.02 us
  local copies, waits for them, and re-layouts: 5.2 us -> 2.51 us
    pallas_call x2, Pallas kernels: 101 us -> 71.9 us  [the longest x1 46.6 us: mlp_square(): pl.pallas_call(mlp_square_kernel, out_shape=jax.ShapeDtypeStruct((rows, m...]
    reduce_sum x4 -> x1, other arithmetic: 2.32 us -> 0.15 us  [most_crossing(): counts = jnp.sum(jnp.stack([right, left]).astype(jnp.int32), axis=2)]
    concatenate x1 -> x0, other arithmetic: 1.95 us -> none  [route_choice(): jnp.concatenate([choices[0][None], choices[1], choices[2]])]
where the time goes in v2:
time: 148 us
  Pallas kernels  139 us (94%)
  other arithmetic  5.02 us (3%)
  local copies, waits for them, and re-layouts  2.51 us (2%)
    pallas_call x1, Pallas kernels, gather(): pl.pallas_call(functools.partial(gather_kernel, parts, chips, width, sub)...  67.4 us
    pallas_call x1, Pallas kernels, mlp_square(): pl.pallas_call(mlp_square_kernel, out_shape=jax.ShapeDtypeStruct((rows, m...  46.6 us
    pallas_call x1, Pallas kernels, attention(): pl.pallas_call(functools.partial(attention_kernel, heads, parts), out_sha...  25.3 us

profile of v2, /device:TPU:0, one launch (start us, length us, event | category | flops | bytes accessed | tf_op | source)
XLA Modules:
  0.0 147.8 jit_solution(3746456942956946337)
XLA Ops:
  0.0 0.8 reduce-window_clone.1
  0.8 0.7 subtract_bitcast_fusion
  1.5 0.8 select_reduce_fusion.2
  2.3 0.1 select_reduce_fusion
  2.4 0.1 compare_and_fusion.1
  2.5 0.2 fusion
  2.6 0.6 reduce_max.30
  3.9 0.1 copy.13.refs_5_
  4.1 1.0 multiply_sine_fusion
  5.1 0.5 pad_maximum_fusion.1
  5.6 1.6 %constant_dynamic-slice_fusion = (bf16[2048,64]{1,0:T(8,128)(2,1)S(1)}, bf16[2048,64]{1,0:T(8,128)(2,1)S(1)}) fusion(bf16[2048,256]{1,0:T(8,128)(2,1)} %param.18, s32[]{:T(128)S(6)} %select_n.23, bf16[2048,256]{1,0:T(8,128)(2,1)} %param.17), kind=kLoop, calls=%fused_computation.17 | loop fusion | bytes 1048580 | tf_op jit(solution)/shard_map/dynamic_slice | solution.py:890
  7.1 0.3 pad_maximum_fusion.refs_2_
  7.4 67.6 %conditional.1 = (bf16[512,2048]{1,0:T(8,128)(2,1)S(1)}, bf16[4096,128]{1,0:T(8,128)(2,1)}) conditional(s32[]{:T(128)} %convert_element_type.14, (s32[8]{0:T(128)}, bf16[128,2048]{1,0:T(8,128)(2,1)}, bf16[1024,512]{1,0:T(8,128)(2,1)}) %tuple.13, (s32[8]{0:T(128)}, bf16[128,2048]{1,0:T(8,128)(2,1)}, bf16[1024,512]{1,0:T(8,128)(2,1)}) %tuple.13), branch_computations={%region_4.5_spmd, %region_5.6_spmd} | conditional | bytes 16 | solution.py:879
  7.4 67.4 %gather.3 = (bf16[4,128,2048]{2,1,0:T(8,128)(2,1)S(1)}, bf16[8,512,128]{2,1,0:T(8,128)(2,1)}) custom-call(s32[8]{0:T(128)} %get-tuple-element.22.slot_ref, bf16[128,2048]{1,0:T(8,128)(2,1)} %get-tuple-element.23.tokens, bf16[1024,512]{1,0:T(8,128)(2,1)} %get-tuple-element.24.prefix), custom_call_target="tpu_custom_call" | custom-call | tf_op jit(solution)/shard_map/cond/branch_1_fun/gather/pallas_call | solution.py:366
  75.0 0.0 copy-start
  75.0 25.3 %attention.1 = (bf16[512,256]{1,0:T(8,128)(2,1)S(1)}, bf16[4,256,2048]{2,1,0:T(8,128)(2,1)}) custom-call(bf16[512,2048]{1,0:T(8,128)(2,1)S(1)} %get-tuple-element.31.refs_0_, bf16[2048,256]{1,0:T(8,128)(2,1)} %refs_1_.1, bf16[2048,128]{1,0:T(8,128)(2,1)S(1)} %pad_maximum_fusion.refs_2_, f32[512,128]{1,0:T(8,128)S(1)} %get-tuple-element.43.refs_3_, ...), custom_call_target="tpu_custom_call" | custom-call | tf_op jit(solution)/shard_map/attention/pallas_call | solution.py:555
  100.3 0.0 copy-done
  100.3 46.6 %mlp.1 = bf16[128,2048]{1,0:T(8,128)(2,1)S(1)} custom-call(bf16[512,256]{1,0:T(8,128)(2,1)S(1)} %get-tuple-element.33.att, bf16[4,256,2048]{2,1,0:T(8,128)(2,1)} %get-tuple-element.34.out_w, bf16[128,2048]{1,0:T(8,128)(2,1)S(1)} %copy-done, bf16[2,2048,1280]{2,1,0:T(8,128)(2,1)} %gate_up.1, bf16[1280,2048]{1,0:T(8,128)(2,1)} %down.1), custom_call_target="tpu_custom_call" | custom-call | tf_op jit(solution)/shard_map/mlp/pallas_call | solution.py:806
  147.0 0.8 copy.20
  (3 shorter events, 0.0 us)
Async XLA Ops:
  75.0 25.3 %copy-start = (bf16[128,2048]{1,0:T(8,128)(2,1)S(1)}, bf16[128,2048]{1,0:T(8,128)(2,1)}, u32[]{:S(2)}) copy-start(bf16[128,2048]{1,0:T(8,128)(2,1)} %tokens.1) | copy-start | bytes 1572868

commit v3 on v2

--- a/solution.py
+++ b/solution.py
@@ -13,6 +13,7 @@
 HD = 64
 PLEN = 4096
 LANES = 128
+SKEW = 3
 NEG_FILL = -1e30
 VMEM = pl.BlockSpec(memory_space=pltpu.VMEM)
 SMEM = pl.BlockSpec(memory_space=pltpu.SMEM)
@@ -136,6 +137,8 @@
     chunks = parts * sub
     chunk_rows = prefix.shape[0] // sub
 
+    for ref in (held_l, held_r):
+        ref[...] = jnp.zeros_like(ref)
     barrier = pltpu.get_barrier_semaphore()
     for d in range(1, parts):
         pl.semaphore_signal(
@@ -244,34 +247,64 @@
         block = own.at[core, pl.ds(m * sub, sub)]
         return lane_copy(block, block, own_send.at[m], own_recv.at[m], sibling)
 
-    def flow(k, has_from, has_to, to, base, held, stage, send, recv, f_send, f_recv):
-        def hop(w):
+    last = chips - 1
+
+    def flow(place, to, base, held, stage, send, recv, f_send, f_recv):
+        def hop(w, k):
             return lane_copy(
                 stage.at[w, k], held.at[w * 2 + core, k], send.at[w, k], recv.at[w, k], to
             )
 
-        def forward(w):
+        def forward(w, k):
             ref = held.at[w * 2 + core, k]
             return lane_copy(ref, ref, f_send.at[w, k], f_recv.at[w, k], sibling)
 
-        @pl.when(has_from)
-        def _():
+        def comes(w):
+            return (place > w) & (place <= last - w)
+
+        def goes(w):
+            return (place >= w) & (place < last - w)
+
+        def receive(s):
+            k = s - SKEW * place
             for w in range(width):
-                hop(w).wait_recv()
-                forward(w).start()
+                @pl.when((k >= 0) & (k < chunks) & comes(w))
+                def _(w=w):
+                    hop(w, k).wait_recv()
+                    forward(w, k).start()
+
+        def pass_on(s):
+            k = s - 1 - SKEW * place
             for w in range(width):
-                forward(w).wait_recv()
-
-        @pl.when(has_to)
-        def _():
+                @pl.when((k >= 0) & (k < chunks) & comes(w))
+                def _(w=w):
+                    forward(w, k).wait_recv()
             for w in range(width):
-                stage[w, k] = pick(
-                    choice[base + w],
-                    [own[0, k], own[1, k]] + [held[i, k] for i in range(2 * width)],
-                )
-                hop(w).start()
-
-    last = chips - 1
+                @pl.when((k >= 0) & (k < chunks) & goes(w))
+                def _(w=w):
+                    stage[w, k] = pick(
+                        choice[base + w],
+                        [own[0, k], own[1, k]] + [held[i, k] for i in range(2 * width)],
+                    )
+                    hop(w, k).start()
+
+        def drain(k):
+            for w in range(width):
+                @pl.when(goes(w))
+                def _(w=w):
+                    hop(w, k).wait_send()
+                @pl.when(comes(w))
+                def _(w=w):
+                    forward(w, k).wait_send()
+
+        return receive, pass_on, drain
+
+    flows = (
+        flow(chip, lax.rem(group + 2, groups), 1,
+             held_l, stage_r, r_send, r_recv, rf_send, rf_recv),
+        flow(last - chip, lax.rem(group + groups - 2, groups), 1 + width,
+             held_r, stage_l, l_send, l_recv, lf_send, lf_recv),
+    )
 
     def step(s, carry):
         m = s // sub
@@ -290,36 +323,22 @@
                 ).wait_recv()
 
             own_copy(m).start()
-            own_copy(m).wait_recv()
-            pl.when(m == parts - 1)(ag_start)
-
-        k = s - chip
-
-        @pl.when((k >= 0) & (k < chunks))
+            pl.when(m == parts // 2)(ag_start)
+
+        for receive, _, _ in flows:
+            receive(s)
+        before = s - 1
+
+        @pl.when((before >= 0) & (before // sub < parts) & (before % sub == 0))
         def _():
-            flow(
-                k, chip > 0, chip < last, lax.rem(group + 2, groups), 1,
-                held_l, stage_r, r_send, r_recv, rf_send, rf_recv,
-            )
-
-        j = s - (last - chip)
-
-        @pl.when((j >= 0) & (j < chunks))
-        def _():
-            flow(
-                j, chip < last, chip > 0, lax.rem(group + groups - 2, groups), 1 + width,
-                held_r, stage_l, l_send, l_recv, lf_send, lf_recv,
-            )
-
-        pl.when(s == chunks + last - 2)(ag_forward)
+            own_copy(before // sub).wait_recv()
+
+        for _, pass_on, _ in flows:
+            pass_on(s)
+        pl.when(s == parts * sub - 1)(ag_forward)
         return carry
 
-    for edge in ((chip == 0, held_l), (chip == last, held_r)):
-        def clear(ref=edge[1]):
-            ref[...] = jnp.zeros_like(ref)
-        pl.when(edge[0])(clear)
-
-    lax.fori_loop(0, chunks + last, step, 0)
+    lax.fori_loop(0, chunks + SKEW * last + 1, step, 0)
 
     def finish(k, carry):
         kv_out[k] = pick(
@@ -333,18 +352,8 @@
     lax.fori_loop(0, chunks, finish, 0)
 
     def drain(k, carry):
-        def one(sem, has):
-            @pl.when(has)
-            def _():
-                for w in range(width):
-                    lane_copy(
-                        stage_r.at[w, k], stage_r.at[w, k], sem.at[w, k], sem.at[w, k], sibling
-                    ).wait_send()
-
-        one(r_send, chip < last)
-        one(l_send, chip > 0)
-        one(rf_send, chip > 0)
-        one(lf_send, chip < last)
+        for _, _, end in flows:
+            end(k)
         return carry
 
     lax.fori_loop(0, chunks, drain, 0)
@@ -358,7 +367,7 @@
 def gather(slots, tokens, prefix, parts, chips, width, identity):
     rows, model = tokens.shape
     shard = prefix.shape[0]
-    sub = 2 if shard >= 512 else 1
+    sub = 4 if shard >= 1024 else 2
     chunks = parts * sub
     piece = (chunks, shard // sub, LANES)
     dma = pltpu.SemaphoreType.DMA

time: 148 us -> 136 us (0.919)
  Pallas kernels: 139 us -> 127 us
    pallas_call x1, Pallas kernels: 67.4 us -> 53.7 us  [gather(): pl.pallas_call(functools.partial(gather_kernel, parts, chips, width, sub)...]
where the time goes in v3:
time: 136 us; the launch traced here: 135 us
  Pallas kernels  127 us (93%)
  other arithmetic  5.02 us (4%)
  local copies, waits for them, and re-layouts  2.51 us (2%)
    pallas_call x1, Pallas kernels, gather(): pl.pallas_call(functools.partial(gather_kernel, parts, chips, width, sub)...  53.7 us
    pallas_call x1, Pallas kernels, mlp_square(): pl.pallas_call(mlp_square_kernel, out_shape=jax.ShapeDtypeStruct((rows, m...  46.8 us
    pallas_call x1, Pallas kernels, attention(): pl.pallas_call(functools.partial(attention_kernel, heads, parts), out_sha...  26.5 us

profile of v3, /device:TPU:0, one launch (start us, length us, event | category | flops | bytes accessed | tf_op | source)
XLA Modules:
  0.0 135.5 jit_solution(4079077697061652762)
XLA Ops:
  0.0 0.8 reduce-window_clone.1
  0.8 0.7 subtract_bitcast_fusion
  1.5 0.8 select_reduce_fusion.2
  2.3 0.1 select_reduce_fusion
  2.4 0.1 compare_and_fusion.1
  2.5 0.2 fusion
  2.6 0.6 reduce_max.30
  3.9 0.1 copy.13.refs_5_
  4.1 1.0 multiply_sine_fusion
  5.1 0.5 pad_maximum_fusion.1
  5.6 1.6 %constant_dynamic-slice_fusion = (bf16[2048,64]{1,0:T(8,128)(2,1)S(1)}, bf16[2048,64]{1,0:T(8,128)(2,1)S(1)}) fusion(bf16[2048,256]{1,0:T(8,128)(2,1)} %param.18, s32[]{:T(128)S(6)} %select_n.23, bf16[2048,256]{1,0:T(8,128)(2,1)} %param.17), kind=kLoop, calls=%fused_computation.17 | loop fusion | bytes 1048580 | tf_op jit(solution)/shard_map/dynamic_slice | solution.py:899
  7.1 0.3 pad_maximum_fusion.refs_2_
  7.4 53.9 %conditional.1 = (bf16[512,2048]{1,0:T(8,128)(2,1)S(1)}, bf16[4096,128]{1,0:T(8,128)(2,1)}) conditional(s32[]{:T(128)} %convert_element_type.14, (s32[8]{0:T(128)}, bf16[128,2048]{1,0:T(8,128)(2,1)}, bf16[1024,512]{1,0:T(8,128)(2,1)}) %tuple.13, (s32[8]{0:T(128)}, bf16[128,2048]{1,0:T(8,128)(2,1)}, bf16[1024,512]{1,0:T(8,128)(2,1)}) %tuple.13), branch_computations={%region_4.5_spmd, %region_5.6_spmd} | conditional | bytes 16 | solution.py:888
  7.4 53.7 %gather.3 = (bf16[4,128,2048]{2,1,0:T(8,128)(2,1)S(1)}, bf16[16,256,128]{2,1,0:T(8,128)(2,1)}) custom-call(s32[8]{0:T(128)} %get-tuple-element.22.slot_ref, bf16[128,2048]{1,0:T(8,128)(2,1)} %get-tuple-element.23.tokens, bf16[1024,512]{1,0:T(8,128)(2,1)} %get-tuple-element.24.prefix), custom_call_target="tpu_custom_call" | custom-call | tf_op jit(solution)/shard_map/cond/branch_1_fun/gather/pallas_call | solution.py:375
  61.3 0.0 copy-start
  61.3 26.5 %attention.1 = (bf16[512,256]{1,0:T(8,128)(2,1)S(1)}, bf16[4,256,2048]{2,1,0:T(8,128)(2,1)}) custom-call(bf16[512,2048]{1,0:T(8,128)(2,1)S(1)} %get-tuple-element.31.refs_0_, bf16[2048,256]{1,0:T(8,128)(2,1)} %refs_1_.1, bf16[2048,128]{1,0:T(8,128)(2,1)S(1)} %pad_maximum_fusion.refs_2_, f32[512,128]{1,0:T(8,128)S(1)} %get-tuple-element.43.refs_3_, ...), custom_call_target="tpu_custom_call" | custom-call | tf_op jit(solution)/shard_map/attention/pallas_call | solution.py:564
  87.9 0.0 copy-done
  87.9 46.8 %mlp.1 = bf16[128,2048]{1,0:T(8,128)(2,1)S(1)} custom-call(bf16[512,256]{1,0:T(8,128)(2,1)S(1)} %get-tuple-element.33.att, bf16[4,256,2048]{2,1,0:T(8,128)(2,1)} %get-tuple-element.34.out_w, bf16[128,2048]{1,0:T(8,128)(2,1)S(1)} %copy-done, bf16[2,2048,1280]{2,1,0:T(8,128)(2,1)} %gate_up.1, bf16[1280,2048]{1,0:T(8,128)(2,1)} %down.1), custom_call_target="tpu_custom_call" | custom-call | tf_op jit(solution)/shard_map/mlp/pallas_call | solution.py:815
  134.7 0.8 copy.20
  (3 shorter events, 0.0 us)
Async XLA Ops:
  61.3 26.5 %copy-start = (bf16[128,2048]{1,0:T(8,128)(2,1)S(1)}, bf16[128,2048]{1,0:T(8,128)(2,1)}, u32[]{:S(2)}) copy-start(bf16[128,2048]{1,0:T(8,128)(2,1)} %tokens.1) | copy-start | bytes 1572868

commit v4 on v3

--- a/solution.py
+++ b/solution.py
@@ -28,24 +28,6 @@
     floats = inputs.astype(F32)
     mean = jnp.mean(floats * floats, axis=-1, keepdims=True)
     return (floats * lax.rsqrt(mean + 1e-05)).astype(BF16)
-
-
-def token_layout(lengths, total_rows):
-    ends_at = jnp.cumsum(lengths)
-    starts_at = ends_at - lengths
-    indices = jnp.arange(total_rows, dtype=jnp.int32)
-    begins = jnp.max(
-        jnp.where(starts_at[None, :] <= indices[:, None], starts_at[None, :], 0), axis=1
-    )
-    return ((PLEN + indices - begins).astype(F32), begins)
-
-
-def rope_tables(positions):
-    halves = HD // 2
-    steps_float = jnp.arange(halves, dtype=F32)
-    inverse = jnp.exp(steps_float * (-2.0 * math.log(10000.0) / HD))
-    angles = positions[:, None] * inverse[None, :]
-    return (jnp.cos(angles), jnp.sin(angles))
 
 
 def most_crossing(group_prefix, chips):
@@ -121,13 +103,16 @@
     return result
 
 
-def gather_kernel(
-    parts, chips, width, sub,
+def gather_kernel(parts, chips, width, sub, *refs):
+    if parts == 4:
+        ow, ow_all, w_send, w_recv, share_send, share_recv = refs[3], refs[6], *refs[-4:]
+        refs = refs[:3] + refs[4:6] + refs[7:-4]
+    (
     slot_ref, tokens, prefix, segment, kv_out,
     packed, own, held_l, held_r, stage_r, stage_l, ag,
     ag_send, ag_recv, a2a_send, a2a_recv, own_send, own_recv,
     r_send, r_recv, l_send, l_recv, rf_send, rf_recv, lf_send, lf_recv,
-):
+    ) = refs
     me = lax.axis_index("tensor")
     group = lax.axis_index("dp")
     chip, core = group // 2, group % 2
@@ -237,6 +222,58 @@
             for d in range(1, parts):
                 ag_copy(d).wait_send()
 
+    def weight_piece(src, place, half, to):
+        quarter = ow.shape[0] // 4
+        at = pl.ds((2 * core + half) * quarter, quarter)
+        return pltpu.make_async_remote_copy(
+            src_ref=ow.at[at] if src == 0 else ow_all.at[src, at],
+            dst_ref=ow_all.at[place, at],
+            send_sem=w_send.at[2 * place + half - 2],
+            recv_sem=w_recv.at[2 * place + half - 2],
+            device_id={"tensor": to},
+            device_id_type=MESH,
+        )
+
+    def share(place):
+        quarter = ow.shape[0] // 4
+        ref = ow_all.at[place, pl.ds(2 * core * quarter, 2 * quarter)]
+        return pltpu.make_async_remote_copy(
+            src_ref=ref, dst_ref=ref, send_sem=share_send.at[place - 1],
+            recv_sem=share_recv.at[place - 1], device_id={"dp": sibling}, device_id_type=MESH,
+        )
+
+    def weight_start():
+        weight_piece(0, 1, 0, near_x).start()
+        weight_piece(0, 2, 1, near_y).start()
+        weight_piece(0, 1, 1, near_x).start()
+        weight_piece(0, 2, 0, near_y).start()
+        ow_all[0] = ow[...]
+
+    def weight_forward():
+        weight_piece(0, 1, 0, near_x).wait_recv()
+        weight_piece(1, 3, 0, near_y).start()
+        weight_piece(0, 2, 1, near_y).wait_recv()
+        weight_piece(2, 3, 1, near_x).start()
+
+    def weight_share():
+        weight_piece(0, 1, 1, near_x).wait_recv()
+        share(1).start()
+        weight_piece(0, 2, 0, near_y).wait_recv()
+        share(2).start()
+
+    def weight_finish():
+        weight_piece(1, 3, 0, near_y).wait_recv()
+        weight_piece(2, 3, 1, near_x).wait_recv()
+        share(3).start()
+
+    def weight_end():
+        for place in (1, 2, 3):
+            share(place).wait_recv()
+        for place in (1, 2, 3):
+            share(place).wait_send()
+            for half in range(2):
+                weight_piece(0, place, half, near_x).wait_send()
+
     def lane_copy(src, dst, send_sem, recv_sem, to):
         return pltpu.make_async_remote_copy(
             src_ref=src, dst_ref=dst, send_sem=send_sem, recv_sem=recv_sem,
@@ -323,7 +360,7 @@
                 ).wait_recv()
 
             own_copy(m).start()
-            pl.when(m == parts // 2)(ag_start)
+            pl.when(m == 1)(ag_start)
 
         for receive, _, _ in flows:
             receive(s)
@@ -335,10 +372,17 @@
 
         for _, pass_on, _ in flows:
             pass_on(s)
-        pl.when(s == parts * sub - 1)(ag_forward)
+        if parts == 4:
+            pl.when(s == 10)(ag_forward)
+            pl.when(s == 10)(weight_start)
+            pl.when(s == 19)(weight_forward)
+            pl.when(s == 23)(weight_share)
         return carry
 
     lax.fori_loop(0, chunks + SKEW * last + 1, step, 0)
+
+    if parts == 4:
+        weight_finish()
 
     def finish(k, carry):
         kv_out[k] = pick(
@@ -362,9 +406,11 @@
     for copy in copies:
         copy.wait_send()
     ag_finish()
-
-
-def gather(slots, tokens, prefix, parts, chips, width, identity):
+    if parts == 4:
+        weight_end()
+
+
+def gather(slots, tokens, prefix, out_w, parts, chips, width, identity):
     rows, model = tokens.shape
     shard = prefix.shape[0]
     sub = 4 if shard >= 1024 else 2
@@ -372,14 +418,21 @@
     piece = (chunks, shard // sub, LANES)
     dma = pltpu.SemaphoreType.DMA
     lane = [dma((width, chunks))] * 8
-    segment, kv = pl.pallas_call(
+    shapes = [
+        jax.ShapeDtypeStruct((parts, rows, model), BF16),
+        jax.ShapeDtypeStruct(piece, BF16),
+    ]
+    operands = [slots, tokens, prefix]
+    extra = []
+    if parts == 4:
+        operands.append(out_w)
+        shapes.append(jax.ShapeDtypeStruct((parts,) + out_w.shape, BF16))
+        extra = [dma((6,))] * 2 + [dma((3,))] * 2
+    segment, kv, *weight = pl.pallas_call(
         functools.partial(gather_kernel, parts, chips, width, sub),
-        out_shape=(
-            jax.ShapeDtypeStruct((parts, rows, model), BF16),
-            jax.ShapeDtypeStruct(piece, BF16),
-        ),
-        in_specs=[SMEM, VMEM, VMEM],
-        out_specs=(VMEM, VMEM),
+        out_shape=shapes,
+        in_specs=[SMEM] + [VMEM] * (len(operands) - 1),
+        out_specs=[VMEM] * len(shapes),
         scratch_shapes=[
             pltpu.VMEM((KVH, sub, shard // sub, LANES), BF16),
             pltpu.VMEM((2,) + piece, BF16),
@@ -391,55 +444,18 @@
         ]
         + [dma((max(parts, 6),))] * 2
         + [dma((parts,))] * 4
-        + lane,
+        + lane
+        + extra,
         compiler_params=pltpu.CompilerParams(
             collective_id=identity, has_side_effects=True, vmem_limit_bytes=52 * MIB
         ),
         name="gather",
-    )(slots, tokens, prefix)
-    return segment.reshape(parts * rows, model), kv.reshape(PLEN, LANES)
-
-
-def attention_kernel(heads, parts, *refs):
-    (x_ref, wq_ref, wkv_ref, cos_ref, sin_ref, begin_ref, kv_ref) = refs[:7]
-    if parts == 4:
-        ow, out_ref, ow_all, queries, keys, values, scores, w_send, w_recv, s_send, s_recv = refs[7:]
-        me = lax.axis_index("tensor")
-        group = lax.axis_index("dp")
-        core = group % 2
-        sibling = group + 1 - 2 * core
-        near_x, near_y = me + 1 - 2 * (me % 2), lax.rem(me + 2, parts)
-        quarter = ow.shape[0] // 4
-
-        def piece(src, place, half, to):
-            at = pl.ds((2 * core + half) * quarter, quarter)
-            return pltpu.make_async_remote_copy(
-                src_ref=ow.at[at] if src == 0 else ow_all.at[src, at],
-                dst_ref=ow_all.at[place, at],
-                send_sem=w_send.at[2 * place + half - 2],
-                recv_sem=w_recv.at[2 * place + half - 2],
-                device_id={"tensor": to},
-                device_id_type=MESH,
-            )
-
-        def share(place):
-            ref = ow_all.at[place, pl.ds(2 * core * quarter, 2 * quarter)]
-            return pltpu.make_async_remote_copy(
-                src_ref=ref, dst_ref=ref, send_sem=s_send.at[place - 1],
-                recv_sem=s_recv.at[place - 1], device_id={"dp": sibling}, device_id_type=MESH,
-            )
-
-        barrier = pltpu.get_barrier_semaphore()
-        for to in ({"tensor": near_x}, {"tensor": near_y}, {"dp": sibling}):
-            pl.semaphore_signal(barrier, inc=1, device_id=to, device_id_type=MESH)
-        pl.semaphore_wait(barrier, 3)
-        piece(0, 1, 0, near_x).start()
-        piece(0, 2, 1, near_y).start()
-        piece(0, 1, 1, near_x).start()
-        piece(0, 2, 0, near_y).start()
-        ow_all[0] = ow[...]
-    else:
-        out_ref, queries, keys, values, scores = refs[7:]
+    )(*operands)
+    return [segment.reshape(parts * rows, model), kv.reshape(PLEN, LANES)] + weight
+
+
+def attention_kernel(heads, x_ref, wq_ref, wk_ref, wv_ref, lengths, kv_ref,
+                     out_ref, queries, keys, values, scores, begin_ref):
     rows = x_ref.shape[0]
     lane = lax.broadcasted_iota(jnp.int32, (1, LANES), 1)
     former = (lane % HD) < HD // 2
@@ -451,9 +467,20 @@
         )
         return tile * cos_table + swapped * sin_table
 
+    index = lax.broadcasted_iota(jnp.int32, (rows, LANES), 0)
+    begins = jnp.zeros((rows, LANES), jnp.int32)
+    start = jnp.int32(0)
+    for r in range(lengths.shape[1]):
+        begins = jnp.where(index >= start, start, begins)
+        start = start + lengths[0, r]
+    begin_ref[...] = begins
+    steps_float = (lane % (HD // 2)).astype(F32)
+    inverse = jnp.exp(steps_float * (-2.0 * math.log(10000.0) / HD))
+    angles = (PLEN + index - begins).astype(F32) * inverse
+    cos_table, sin_table = jnp.cos(angles), jnp.sin(angles)
+
     x = x_ref[...]
     mapped = jnp.dot(x, wq_ref[...], preferred_element_type=F32)
-    cos_table, sin_table = cos_ref[...], sin_ref[...]
     for h in range(heads):
         if h % 2 == 0:
             tile = mapped[:, (h // 2) * LANES : (h // 2 + 1) * LANES]
@@ -462,8 +489,13 @@
         else:
             head = pltpu.roll(tile, HD, 1)
         queries[h] = jnp.where(low, head, 0.0).astype(BF16)
-    pair = jnp.dot(x, wkv_ref[...], preferred_element_type=F32)
-    pair = jnp.where(low, rotated(pair, cos_table, sin_table), pair)
+    is_odd = (lax.axis_index("tensor") * heads // (QH // KVH)) % 2 == 1
+    new_k = jnp.dot(x, wk_ref[...], preferred_element_type=F32)
+    new_v = jnp.dot(x, wv_ref[...], preferred_element_type=F32)
+    new_k = rotated(new_k, cos_table, sin_table)
+    new_k = jnp.where(is_odd, pltpu.roll(new_k, HD, 1), new_k)
+    new_v = jnp.where(is_odd, new_v, pltpu.roll(new_v, HD, 1))
+    pair = jnp.where(low, new_k, new_v)
     keys[0:PLEN, :] = kv_ref[...]
     keys[PLEN:, :] = pair.astype(BF16)
     values[...] = jnp.where(low, 1.0, keys[...].astype(F32)).astype(BF16)
@@ -500,21 +532,6 @@
         return blended
 
     def one(i, carry):
-        if parts == 4:
-            @pl.when(i == 1)
-            def _():
-                piece(0, 1, 0, near_x).wait_recv()
-                piece(1, 3, 0, near_y).start()
-                piece(0, 2, 1, near_y).wait_recv()
-                piece(2, 3, 1, near_x).start()
-
-            @pl.when(i == pairs * per_head - 1)
-            def _():
-                piece(0, 1, 1, near_x).wait_recv()
-                share(1).start()
-                piece(0, 2, 0, near_y).wait_recv()
-                share(2).start()
-
         p, b = i // per_head, i % per_head
         start = pl.multiple_of(b * block, block)
         even = one_head(2 * p, start, 0)
@@ -529,47 +546,31 @@
         return carry
 
     lax.fori_loop(0, pairs * per_head, one, 0)
-    if parts == 4:
-        piece(1, 3, 0, near_y).wait_recv()
-        piece(2, 3, 1, near_x).wait_recv()
-        share(3).start()
-        for place in (1, 2, 3):
-            share(place).wait_recv()
-        for place in (1, 2, 3):
-            share(place).wait_send()
-            for half in range(2):
-                piece(0, place, half, near_x).wait_send()
-
-
-def attention(x, wq, wkv, cos_table, sin_table, begins, kv, out_w, heads, parts, identity):
+
+
+def attention(x, wq, key_weight, value_weight, lengths, kv, heads, tile):
     rows = x.shape[0]
     total = PLEN + rows
     block = 256 if rows % 256 == 0 else rows
+    columns = pl.BlockSpec((wq.shape[0], LANES), lambda i: (0, tile()))
+    whole = lambda shape: pl.BlockSpec(shape, lambda i: (0,) * len(shape))
     width = (heads + 1) // 2 * LANES
-    exchange = parts == 4
-    shapes = [jax.ShapeDtypeStruct((rows, width), BF16)]
-    operands = [x, wq, wkv, cos_table, sin_table, begins, kv]
-    scratch = [
-        pltpu.VMEM((heads, rows, LANES), BF16),
-        pltpu.VMEM((total, LANES), BF16),
-        pltpu.VMEM((total, LANES), BF16),
-        pltpu.VMEM((2, block, total), F32),
-    ]
-    params = dict(vmem_limit_bytes=52 * MIB)
-    if exchange:
-        operands.append(out_w)
-        shapes.append(jax.ShapeDtypeStruct((parts,) + out_w.shape, BF16))
-        scratch += [pltpu.SemaphoreType.DMA((6,))] * 2 + [pltpu.SemaphoreType.DMA((3,))] * 2
-        params.update(collective_id=identity, has_side_effects=True)
     return pl.pallas_call(
-        functools.partial(attention_kernel, heads, parts),
-        out_shape=shapes,
-        in_specs=[VMEM] * len(operands),
-        out_specs=[VMEM] * len(shapes),
-        scratch_shapes=scratch,
-        compiler_params=pltpu.CompilerParams(**params),
+        functools.partial(attention_kernel, heads),
+        grid=(1,),
+        out_shape=jax.ShapeDtypeStruct((rows, width), BF16),
+        in_specs=[whole(x.shape), whole(wq.shape), columns, columns, SMEM, whole(kv.shape)],
+        out_specs=whole((rows, width)),
+        scratch_shapes=[
+            pltpu.VMEM((heads, rows, LANES), BF16),
+            pltpu.VMEM((total, LANES), BF16),
+            pltpu.VMEM((total, LANES), BF16),
+            pltpu.VMEM((2, block, total), F32),
+            pltpu.VMEM((rows, LANES), jnp.int32),
+        ],
+        compiler_params=pltpu.CompilerParams(vmem_limit_bytes=52 * MIB),
         name="attention",
-    )(*operands)
+    )(x, wq, key_weight, value_weight, lengths, kv)
 
 
 def mlp_kernel(
@@ -873,45 +874,35 @@
 ):
     parts = lax.axis_size("tensor")
     chips = lax.axis_size("dp") // 2
-    rank = lax.axis_index("tensor")
-    rows = tokens.shape[0] * parts
     heads = query_weight.shape[1] // HD
-    kv_head = rank * heads // (QH // KVH)
 
     most = most_crossing(group_prefix, chips)
 
     def routed(width, identity):
         def run(prefix, rows_in):
-            return gather(group_prefix, rows_in, prefix, parts, chips, width, identity)
+            return gather(
+                group_prefix, rows_in, prefix, out_weight, parts, chips, width, identity
+            )
         return run
 
-    segment, kv = lax.cond(
+    segment, kv, *gathered = lax.cond(
         most <= 2, routed(1, 0), routed(chips // 2, 1), prefix_cache, tokens
     )
 
-    positions, begins = token_layout(lengths[0], rows)
-    cos_half, sin_half = rope_tables(positions)
-    cos_table = jnp.concatenate([cos_half] * 4, axis=1)
-    sin_table = jnp.concatenate([sin_half] * 4, axis=1)
-    wkv = jnp.concatenate(
-        [
-            lax.dynamic_slice_in_dim(key_weight, kv_head * HD, HD, 1),
-            lax.dynamic_slice_in_dim(value_weight, kv_head * HD, HD, 1),
-        ],
-        axis=1,
-    )
     wq = query_weight
     if heads % 2:
         wq = jnp.pad(wq, ((0, 0), (0, HD)))
-    outputs = attention(
-        segment, wq, wkv, cos_table, sin_table, begins[:, None], kv, out_weight, heads, parts, 3
-    )
+
+    def tile():
+        return lax.axis_index("tensor") * heads // (QH // KVH) // 2
+
+    att = attention(segment, wq, key_weight, value_weight, lengths, kv, heads, tile)
     if parts == 4:
-        return mlp_square(*outputs, tokens, gate_up_weight, down_weight, 2)
+        return mlp_square(att, gathered[0], tokens, gate_up_weight, down_weight, 2)
     out_w = out_weight
     if heads % 2:
         out_w = jnp.pad(out_w, ((0, HD), (0, 0)))
-    return mlp(outputs[0], out_w, tokens, gate_up_weight, down_weight, parts, 2)
+    return mlp(att, out_w, tokens, gate_up_weight, down_weight, parts, 2)
 
 
 def solution(mesh):

time: 136 us -> 129 us (0.949)
  other arithmetic: 5.02 us -> 1.77 us
  Pallas kernels: 127 us -> 125 us
  local copies, waits for them, and re-layouts: 2.51 us -> 0.81 us
    pallas_call x1, Pallas kernels: 26.5 us -> 18.2 us  [attention(): pl.pallas_call(functools.partial(attention_kernel, heads), grid=(1,), out...]
    pallas_call x1, Pallas kernels: 53.7 us -> 60.1 us  [gather(): pl.pallas_call(functools.partial(gather_kernel, parts, chips, width, sub)...]
    dynamic_slice x1 -> x0, local copies, waits for them, and re-layouts: 1.56 us -> none  [on_device(): lax.dynamic_slice_in_dim(value_weight, kv_head * HD, HD, 1)]
where the time goes in v4:
time: 129 us; the launch traced here: 128 us
  Pallas kernels  125 us (97%)
  other arithmetic  1.77 us (1%)
    pallas_call x1, Pallas kernels, gather(): pl.pallas_call(functools.partial(gather_kernel, parts, chips, width, sub)...  60.1 us
    pallas_call x1, Pallas kernels, mlp_square(): pl.pallas_call(mlp_square_kernel, out_shape=jax.ShapeDtypeStruct((rows, m...  46.7 us
    pallas_call x1, Pallas kernels, attention(): pl.pallas_call(functools.partial(attention_kernel, heads), grid=(1,), out...  18.2 us

profile of v4, /device:TPU:0, one launch (start us, length us, event | category | flops | bytes accessed | tf_op | source)
XLA Modules:
  0.0 128.5 jit_solution(11576211886546283078)
XLA Ops:
  0.0 0.0 copy-start
  0.0 0.0 copy-start.1
  0.0 0.9 select_reduce_fusion.1
  0.9 0.1 compare_and_fusion.1
  1.0 0.2 fusion
  1.1 0.6 reduce_max.19
  2.4 60.3 %conditional.1 = (bf16[512,2048]{1,0:T(8,128)(2,1)S(1)}, bf16[4096,128]{1,0:T(8,128)(2,1)}, bf16[4,256,2048]{2,1,0:T(8,128)(2,1)}) conditional(s32[]{:T(128)} %convert_element_type.7, (s32[8]{0:T(128)}, bf16[128,2048]{1,0:T(8,128)(2,1)}, bf16[1024,512]{1,0:T(8,128)(2,1)}, bf16[256,2048]{1,0:T(8,128)(2,1)}) %tuple.13, (s32[8]{0:T(128)}, ...), branch_computations={%region_4.5_spmd, %region_5.6_spmd} | conditional | bytes 24 | solution.py:888
  2.5 60.1 %gather.3 = (bf16[4,128,2048]{2,1,0:T(8,128)(2,1)S(1)}, bf16[16,256,128]{2,1,0:T(8,128)(2,1)}, bf16[4,256,2048]{2,1,0:T(8,128)(2,1)}) custom-call(s32[8]{0:T(128)} %get-tuple-element.28.refs_0_, bf16[128,2048]{1,0:T(8,128)(2,1)} %get-tuple-element.29.refs_1_, bf16[1024,512]{1,0:T(8,128)(2,1)} %get-tuple-element.30.refs_2_, ...), custom_call_target="tpu_custom_call" | custom-call | tf_op jit(solution)/shard_map/cond/branch_1_fun/gather/pallas_call | solution.py:431
  62.7 0.0 copy-start.2
  62.7 0.0 copy-done
  62.8 0.0 copy-done.1
  62.8 18.2 %attention.1.att = bf16[512,256]{1,0:T(8,128)(2,1)S(1)} custom-call(bf16[512,2048]{1,0:T(8,128)(2,1)S(1)} %get-tuple-element.38.x_ref, bf16[2048,256]{1,0:T(8,128)(2,1)S(1)} %copy-done, bf16[2048,256]{1,0:T(8,128)(2,1)} %wk_ref.1, bf16[2048,256]{1,0:T(8,128)(2,1)} %wv_ref.1, s32[1,8]{1,0:T(1,128)S(1)} %copy-done.1, bf16[4096,128]{1,0:T(8,128)(2,1)} %get-tuple-element.39.kv_ref), custom_call_target="tpu_custom_call" | custom-call | tf_op jit(solution)/shard_map/attention/pallas_call | solution.py:558
  81.0 0.0 copy-done.2
  81.0 46.7 %mlp.1 = bf16[128,2048]{1,0:T(8,128)(2,1)S(1)} custom-call(bf16[512,256]{1,0:T(8,128)(2,1)S(1)} %attention.1.att, bf16[4,256,2048]{2,1,0:T(8,128)(2,1)} %get-tuple-element.40.out_w, bf16[128,2048]{1,0:T(8,128)(2,1)S(1)} %copy-done.2, bf16[2,2048,1280]{2,1,0:T(8,128)(2,1)} %gate_up.1, bf16[1280,2048]{1,0:T(8,128)(2,1)} %down.1), custom_call_target="tpu_custom_call" | custom-call | tf_op jit(solution)/shard_map/mlp/pallas_call | solution.py:816
  127.7 0.8 copy.20
  (1 shorter events, 0.0 us)
Async XLA Ops:
  0.0 62.8 %copy-start = (bf16[2048,256]{1,0:T(8,128)(2,1)S(1)}, bf16[2048,256]{1,0:T(8,128)(2,1)}, u32[]{:S(2)}) copy-start(bf16[2048,256]{1,0:T(8,128)(2,1)} %wq_ref.1) | copy-start | bytes 3145732
  0.0 62.8 %copy-start.1 = (s32[1,8]{1,0:T(1,128)S(1)}, s32[1,8]{1,0:T(1,128)}, u32[]{:S(2)}) copy-start(s32[1,8]{1,0:T(1,128)} %lengths.1) | copy-start | bytes 100
  62.7 18.3 %copy-start.2 = (bf16[128,2048]{1,0:T(8,128)(2,1)S(1)}, bf16[128,2048]{1,0:T(8,128)(2,1)}, u32[]{:S(2)}) copy-start(bf16[128,2048]{1,0:T(8,128)(2,1)} %tokens.1) | copy-start | bytes 1572868

commit v5 on v4

--- a/solution.py
+++ b/solution.py
@@ -223,10 +223,10 @@
                 ag_copy(d).wait_send()
 
     def weight_piece(src, place, half, to):
-        quarter = ow.shape[0] // 4
+        quarter, moved = ow.shape[0] // 4, ow_all.shape[2]
         at = pl.ds((2 * core + half) * quarter, quarter)
         return pltpu.make_async_remote_copy(
-            src_ref=ow.at[at] if src == 0 else ow_all.at[src, at],
+            src_ref=ow.at[at, 0:moved] if src == 0 else ow_all.at[src, at],
             dst_ref=ow_all.at[place, at],
             send_sem=w_send.at[2 * place + half - 2],
             recv_sem=w_recv.at[2 * place + half - 2],
@@ -247,7 +247,7 @@
         weight_piece(0, 2, 1, near_y).start()
         weight_piece(0, 1, 1, near_x).start()
         weight_piece(0, 2, 0, near_y).start()
-        ow_all[0] = ow[...]
+        ow_all[0] = ow[:, 0 : ow_all.shape[2]]
 
     def weight_forward():
         weight_piece(0, 1, 0, near_x).wait_recv()
@@ -426,7 +426,7 @@
     extra = []
     if parts == 4:
         operands.append(out_w)
-        shapes.append(jax.ShapeDtypeStruct((parts,) + out_w.shape, BF16))
+        shapes.append(jax.ShapeDtypeStruct((parts, out_w.shape[0], model // 2), BF16))
         extra = [dma((6,))] * 2 + [dma((3,))] * 2
     segment, kv, *weight = pl.pallas_call(
         functools.partial(gather_kernel, parts, chips, width, sub),
@@ -454,19 +454,9 @@
     return [segment.reshape(parts * rows, model), kv.reshape(PLEN, LANES)] + weight
 
 
-def attention_kernel(heads, x_ref, wq_ref, wk_ref, wv_ref, lengths, kv_ref,
-                     out_ref, queries, keys, values, scores, begin_ref):
-    rows = x_ref.shape[0]
+def table_kernel(lengths, cos_ref, sin_ref, begin_ref):
+    rows = begin_ref.shape[0]
     lane = lax.broadcasted_iota(jnp.int32, (1, LANES), 1)
-    former = (lane % HD) < HD // 2
-    low = lane < HD
-
-    def rotated(tile, cos_table, sin_table):
-        swapped = jnp.where(
-            former, -pltpu.roll(tile, LANES - HD // 2, 1), pltpu.roll(tile, HD // 2, 1)
-        )
-        return tile * cos_table + swapped * sin_table
-
     index = lax.broadcasted_iota(jnp.int32, (rows, LANES), 0)
     begins = jnp.zeros((rows, LANES), jnp.int32)
     start = jnp.int32(0)
@@ -477,8 +467,62 @@
     steps_float = (lane % (HD // 2)).astype(F32)
     inverse = jnp.exp(steps_float * (-2.0 * math.log(10000.0) / HD))
     angles = (PLEN + index - begins).astype(F32) * inverse
-    cos_table, sin_table = jnp.cos(angles), jnp.sin(angles)
-
+    cos_ref[...] = jnp.cos(angles)
+    sin_ref[...] = jnp.sin(angles)
+
+
+def attention_kernel(heads, parts, *refs):
+    (x_ref, wq_ref, wk_ref, wv_ref, cos_ref, sin_ref, begin_ref, kv_ref) = refs[:8]
+    if parts == 4:
+        ow, out_ref, ow_all, queries, keys, values, scores, w_send, w_recv, s_send, s_recv = refs[8:]
+        me = lax.axis_index("tensor")
+        group = lax.axis_index("dp")
+        core = group % 2
+        sibling = group + 1 - 2 * core
+        near_x, near_y = me + 1 - 2 * (me % 2), lax.rem(me + 2, parts)
+        quarter, moved = ow.shape[0] // 4, ow_all.shape[2]
+
+        def piece(src, place, half, to):
+            at = pl.ds((2 * core + half) * quarter, quarter)
+            return pltpu.make_async_remote_copy(
+                src_ref=ow.at[at, pl.ds(moved, moved)] if src == 0 else ow_all.at[src, at],
+                dst_ref=ow_all.at[place, at],
+                send_sem=w_send.at[2 * place + half - 2],
+                recv_sem=w_recv.at[2 * place + half - 2],
+                device_id={"tensor": to},
+                device_id_type=MESH,
+            )
+
+        def share(place):
+            ref = ow_all.at[place, pl.ds(2 * core * quarter, 2 * quarter)]
+            return pltpu.make_async_remote_copy(
+                src_ref=ref, dst_ref=ref, send_sem=s_send.at[place - 1],
+                recv_sem=s_recv.at[place - 1], device_id={"dp": sibling}, device_id_type=MESH,
+            )
+
+        barrier = pltpu.get_barrier_semaphore()
+        for to in ({"tensor": near_x}, {"tensor": near_y}, {"dp": sibling}):
+            pl.semaphore_signal(barrier, inc=1, device_id=to, device_id_type=MESH)
+        pl.semaphore_wait(barrier, 3)
+        piece(0, 1, 0, near_x).start()
+        piece(0, 2, 1, near_y).start()
+        piece(0, 1, 1, near_x).start()
+        piece(0, 2, 0, near_y).start()
+        ow_all[0] = ow[:, moved:]
+    else:
+        out_ref, queries, keys, values, scores = refs[8:]
+    rows = x_ref.shape[0]
+    lane = lax.broadcasted_iota(jnp.int32, (1, LANES), 1)
+    former = (lane % HD) < HD // 2
+    low = lane < HD
+
+    def rotated(tile, cos_table, sin_table):
+        swapped = jnp.where(
+            former, -pltpu.roll(tile, LANES - HD // 2, 1), pltpu.roll(tile, HD // 2, 1)
+        )
+        return tile * cos_table + swapped * sin_table
+
+    cos_table, sin_table = cos_ref[...], sin_ref[...]
     x = x_ref[...]
     mapped = jnp.dot(x, wq_ref[...], preferred_element_type=F32)
     for h in range(heads):
@@ -532,6 +576,27 @@
         return blended
 
     def one(i, carry):
+        if parts == 4:
+            @pl.when(i == 1)
+            def _():
+                piece(0, 1, 0, near_x).wait_recv()
+                piece(1, 3, 0, near_y).start()
+                piece(0, 2, 1, near_y).wait_recv()
+                piece(2, 3, 1, near_x).start()
+
+            @pl.when(i == 2)
+            def _():
+                piece(0, 1, 1, near_x).wait_recv()
+                share(1).start()
+                piece(0, 2, 0, near_y).wait_recv()
+                share(2).start()
+
+            @pl.when(i == pairs * per_head - 1)
+            def _():
+                piece(1, 3, 0, near_y).wait_recv()
+                piece(2, 3, 1, near_x).wait_recv()
+                share(3).start()
+
         p, b = i // per_head, i % per_head
         start = pl.multiple_of(b * block, block)
         even = one_head(2 * p, start, 0)
@@ -546,31 +611,58 @@
         return carry
 
     lax.fori_loop(0, pairs * per_head, one, 0)
-
-
-def attention(x, wq, key_weight, value_weight, lengths, kv, heads, tile):
+    if parts == 4:
+        for place in (1, 2, 3):
+            share(place).wait_recv()
+        for place in (1, 2, 3):
+            share(place).wait_send()
+            for half in range(2):
+                piece(0, place, half, near_x).wait_send()
+
+
+def attention(x, wq, key_weight, value_weight, lengths, kv, out_w, heads, tile, parts, identity):
     rows = x.shape[0]
     total = PLEN + rows
     block = 256 if rows % 256 == 0 else rows
+    table = jax.ShapeDtypeStruct((rows, LANES), F32)
+    tables = pl.pallas_call(
+        table_kernel,
+        out_shape=[table, table, jax.ShapeDtypeStruct((rows, LANES), jnp.int32)],
+        in_specs=[SMEM],
+        out_specs=[VMEM] * 3,
+        name="tables",
+    )(lengths)
     columns = pl.BlockSpec((wq.shape[0], LANES), lambda i: (0, tile()))
     whole = lambda shape: pl.BlockSpec(shape, lambda i: (0,) * len(shape))
-    width = (heads + 1) // 2 * LANES
+    shapes = [jax.ShapeDtypeStruct((rows, (heads + 1) // 2 * LANES), BF16)]
+    operands = [x, wq, key_weight, value_weight, *tables, kv]
+    specs = [whole(x.shape), whole(wq.shape), columns, columns]
+    specs += [whole(t.shape) for t in tables] + [whole(kv.shape)]
+    scratch = [
+        pltpu.VMEM((heads, rows, LANES), BF16),
+        pltpu.VMEM((total, LANES), BF16),
+        pltpu.VMEM((total, LANES), BF16),
+        pltpu.VMEM((2, block, total), F32),
+    ]
+    params = dict(vmem_limit_bytes=52 * MIB)
+    out_specs = [whole(shapes[0].shape)]
+    if parts == 4:
+        operands.append(out_w)
+        specs.append(VMEM)
+        shapes.append(jax.ShapeDtypeStruct((parts, out_w.shape[0], out_w.shape[1] // 2), BF16))
+        out_specs.append(VMEM)
+        scratch += [pltpu.SemaphoreType.DMA((6,))] * 2 + [pltpu.SemaphoreType.DMA((3,))] * 2
+        params.update(collective_id=identity, has_side_effects=True)
     return pl.pallas_call(
-        functools.partial(attention_kernel, heads),
+        functools.partial(attention_kernel, heads, parts),
         grid=(1,),
-        out_shape=jax.ShapeDtypeStruct((rows, width), BF16),
-        in_specs=[whole(x.shape), whole(wq.shape), columns, columns, SMEM, whole(kv.shape)],
-        out_specs=whole((rows, width)),
-        scratch_shapes=[
-            pltpu.VMEM((heads, rows, LANES), BF16),
-            pltpu.VMEM((total, LANES), BF16),
-            pltpu.VMEM((total, LANES), BF16),
-            pltpu.VMEM((2, block, total), F32),
-            pltpu.VMEM((rows, LANES), jnp.int32),
-        ],
-        compiler_params=pltpu.CompilerParams(vmem_limit_bytes=52 * MIB),
+        out_shape=shapes,
+        in_specs=specs,
+        out_specs=out_specs,
+        scratch_shapes=scratch,
+        compiler_params=pltpu.CompilerParams(**params),
         name="attention",
-    )(x, wq, key_weight, value_weight, lengths, kv)
+    )(*operands)
 
 
 def mlp_kernel(
@@ -675,7 +767,7 @@
 
 
 def mlp_square_kernel(
-    att, out_w, tokens, gate_up, down, result,
+    att, out_l, out_r, tokens, gate_up, down, result,
     gu_v, dn_v, att_v, mid_v, rows_v, f_v, f_in, hidden,
     w_sem, as_sem, ar_sem, gs_sem, gr_sem, fs_sem, fr_sem,
 ):
@@ -716,8 +808,11 @@
         copy.start()
 
     def group_term(block, slot):
-        term = jnp.dot(block, out_w[slot], preferred_element_type=F32)
-        return term.astype(BF16).astype(F32)
+        terms = [
+            jnp.dot(block, weight[slot], preferred_element_type=F32).astype(BF16).astype(F32)
+            for weight in (out_l, out_r)
+        ]
+        return jnp.concatenate(terms, axis=1)
 
     total = group_term(att[pl.ds(pl.multiple_of(me * rows, rows), rows), :], 0)
     for copy, slot in zip(swaps[1:] + swaps[:1], (1, 2, 3)):
@@ -808,7 +903,7 @@
             back(1, half, place - 1, near_x).wait_send()
 
 
-def mlp_square(att, out_w, tokens, gate_up, down, identity):
+def mlp_square(att, out_l, out_r, tokens, gate_up, down, identity):
     rows, model = tokens.shape
     parts = 4
     dma = pltpu.SemaphoreType.DMA
@@ -816,7 +911,7 @@
     return pl.pallas_call(
         mlp_square_kernel,
         out_shape=jax.ShapeDtypeStruct((rows, model), BF16),
-        in_specs=[VMEM, VMEM, VMEM, ANY, ANY],
+        in_specs=[VMEM, VMEM, VMEM, VMEM, ANY, ANY],
         out_specs=VMEM,
         scratch_shapes=[
             pltpu.VMEM(gate_up.shape, BF16),
@@ -833,7 +928,7 @@
             collective_id=identity, has_side_effects=True, vmem_limit_bytes=52 * MIB
         ),
         name="mlp",
-    )(att, out_w, tokens, gate_up, down)
+    )(att, out_l, out_r, tokens, gate_up, down)
 
 
 def mlp(att, out_w, tokens, gate_up, down, parts, identity):
@@ -896,9 +991,11 @@
     def tile():
         return lax.axis_index("tensor") * heads // (QH // KVH) // 2
 
-    att = attention(segment, wq, key_weight, value_weight, lengths, kv, heads, tile)
+    att, *rest = attention(
+        segment, wq, key_weight, value_weight, lengths, kv, out_weight, heads, tile, parts, 3
+    )
     if parts == 4:
-        return mlp_square(att, gathered[0], tokens, gate_up_weight, down_weight, 2)
+        return mlp_square(att, *gathered, *rest, tokens, gate_up_weight, down_weight, 2)
     out_w = out_weight
     if heads % 2:
         out_w = jnp.pad(out_w, ((0, HD), (0, 0)))

time: 129 us -> 132 us (1.023)
  local copies, waits for them, and re-layouts: 0.81 us -> 3.65 us
    pallas_call x1 -> x2, Pallas kernels: 18.2 us -> 23.5 us  [the longest x1 20.9 us: attention(): pl.pallas_call(functools.partial(attention_kernel, heads, parts), grid=(1...]
    pallas_call x1, Pallas kernels: 60.1 us -> 55.4 us  [gather(): pl.pallas_call(functools.partial(gather_kernel, parts, chips, width, sub)...]
    unnamed x7 -> x9, local copies, waits for them, and re-layouts: 0.81 us -> 3.65 us
where the time goes in v5:
time: 132 us; the launch traced here: 131 us
  Pallas kernels  125 us (95%)
  local copies, waits for them, and re-layouts  3.65 us (3%)
  other arithmetic  1.68 us (1%)
    pallas_call x1, Pallas kernels, gather(): pl.pallas_call(functools.partial(gather_kernel, parts, chips, width, sub)...  55.4 us
    pallas_call x1, Pallas kernels, mlp_square(): pl.pallas_call(mlp_square_kernel, out_shape=jax.ShapeDtypeStruct((rows, m...  46.3 us
    pallas_call x1, Pallas kernels, attention(): pl.pallas_call(functools.partial(attention_kernel, heads, parts), grid=(1...  20.9 us
    unnamed x9, local copies, waits for them, and re-layouts  3.65 us

profile of v5, /device:TPU:0, one launch (start us, length us, event | category | flops | bytes accessed | tf_op | source)
XLA Modules:
  0.0 131.4 jit_solution(14306481530022268434)
XLA Ops:
  0.0 0.8 select_reduce_fusion.1
  0.8 0.1 compare_and_fusion.1
  0.9 0.1 fusion
  1.0 0.6 reduce_max.19
  2.3 55.6 %conditional.1 = (bf16[512,2048]{1,0:T(8,128)(2,1)S(1)}, bf16[4096,128]{1,0:T(8,128)(2,1)S(1)}, bf16[4,256,1024]{2,1,0:T(8,128)(2,1)}) conditional(s32[]{:T(128)} %convert_element_type.7, (s32[8]{0:T(128)}, bf16[128,2048]{1,0:T(8,128)(2,1)}, bf16[1024,512]{1,0:T(8,128)(2,1)}, bf16[256,2048]{1,0:T(8,128)(2,1)}) %tuple.13, (s32[8]{0:T(128)}, ...), branch_computations={%region_4.5_spmd, %region_5.6_spmd} | conditional | bytes 24 | solution.py:983
  2.4 55.4 %gather.3 = (bf16[4,128,2048]{2,1,0:T(8,128)(2,1)S(1)}, bf16[16,256,128]{2,1,0:T(8,128)(2,1)S(1)}, bf16[4,256,1024]{2,1,0:T(8,128)(2,1)}) custom-call(s32[8]{0:T(128)} %get-tuple-element.28.refs_0_, bf16[128,2048]{1,0:T(8,128)(2,1)} %get-tuple-element.29.refs_1_, bf16[1024,512]{1,0:T(8,128)(2,1)} %get-tuple-element.30.refs_2_, ...), custom_call_target="tpu_custom_call" | custom-call | tf_op jit(solution)/shard_map/cond/branch_1_fun/gather/pallas_call | solution.py:431
  58.0 2.6 %tables.1 = (f32[512,128]{1,0:T(8,128)}, f32[512,128]{1,0:T(8,128)}, s32[512,128]{1,0:T(8,128)}) custom-call(s32[1,8]{1,0:T(1,128)} %lengths.1), custom_call_target="tpu_custom_call" | custom-call | tf_op jit(solution)/shard_map/tables/pallas_call | solution.py:628
  60.6 0.0 copy-start
  60.6 0.9 copy-done
  61.5 0.0 copy-start.1
  61.5 0.9 copy-done.1
  62.5 0.0 copy-start.2
  62.5 0.9 copy-done.2
  63.4 0.0 copy-start.3
  63.4 20.9 %attention.1 = (bf16[512,256]{1,0:T(8,128)(2,1)S(1)}, bf16[4,256,1024]{2,1,0:T(8,128)(2,1)}) custom-call(bf16[512,2048]{1,0:T(8,128)(2,1)S(1)} %get-tuple-element.43.refs_0_, bf16[2048,256]{1,0:T(8,128)(2,1)} %refs_1_.1, bf16[2048,256]{1,0:T(8,128)(2,1)} %refs_2_.1, bf16[2048,256]{1,0:T(8,128)(2,1)} %refs_3_.1, f32[512,128]{1,0:T(8,128)S(1)} %copy-done, ...), custom_call_target="tpu_custom_call" | custom-call | tf_op jit(solution)/shard_map/attention/pallas_call | solution.py:656
  84.3 0.0 copy-done.3
  84.3 46.3 %mlp.1 = bf16[128,2048]{1,0:T(8,128)(2,1)S(1)} custom-call(bf16[512,256]{1,0:T(8,128)(2,1)S(1)} %get-tuple-element.48.att, bf16[4,256,1024]{2,1,0:T(8,128)(2,1)} %get-tuple-element.49.out_l, bf16[4,256,1024]{2,1,0:T(8,128)(2,1)} %get-tuple-element.50.out_r, bf16[128,2048]{1,0:T(8,128)(2,1)S(1)} %copy-done.3, bf16[2,2048,1280]{2,1,0:T(8,128)(2,1)} %gate_up.1, ...), custom_call_target="tpu_custom_call" | custom-call | tf_op jit(solution)/shard_map/mlp/pallas_call | solution.py:911
  130.7 0.8 copy.20
  (1 shorter events, 0.0 us)
Async XLA Ops:
  60.6 1.0 copy-start
  61.5 0.9 copy-start.1
  62.5 0.9 copy-start.2
  63.4 20.9 %copy-start.3 = (bf16[128,2048]{1,0:T(8,128)(2,1)S(1)}, bf16[128,2048]{1,0:T(8,128)(2,1)}, u32[]{:S(2)}) copy-start(bf16[128,2048]{1,0:T(8,128)(2,1)} %tokens.1) | copy-start | bytes 1572868

commit v6 on v5

--- a/solution.py
+++ b/solution.py
@@ -454,9 +454,58 @@
     return [segment.reshape(parts * rows, model), kv.reshape(PLEN, LANES)] + weight
 
 
-def table_kernel(lengths, cos_ref, sin_ref, begin_ref):
-    rows = begin_ref.shape[0]
+def attention_kernel(heads, parts, *refs):
+    (x_ref, wq_ref, wk_ref, wv_ref, lengths, kv_ref) = refs[:6]
+    if parts == 4:
+        (ow, out_ref, ow_all, queries, keys, values, scores, begin_ref,
+         w_send, w_recv, s_send, s_recv) = refs[6:]
+        me = lax.axis_index("tensor")
+        group = lax.axis_index("dp")
+        core = group % 2
+        sibling = group + 1 - 2 * core
+        near_x, near_y = me + 1 - 2 * (me % 2), lax.rem(me + 2, parts)
+        quarter, moved = ow.shape[0] // 4, ow_all.shape[2]
+
+        def piece(src, place, half, to):
+            at = pl.ds((2 * core + half) * quarter, quarter)
+            return pltpu.make_async_remote_copy(
+                src_ref=ow.at[at, pl.ds(moved, moved)] if src == 0 else ow_all.at[src, at],
+                dst_ref=ow_all.at[place, at],
+                send_sem=w_send.at[2 * place + half - 2],
+                recv_sem=w_recv.at[2 * place + half - 2],
+                device_id={"tensor": to},
+                device_id_type=MESH,
+            )
+
+        def share(place):
+            ref = ow_all.at[place, pl.ds(2 * core * quarter, 2 * quarter)]
+            return pltpu.make_async_remote_copy(
+                src_ref=ref, dst_ref=ref, send_sem=s_send.at[place - 1],
+                recv_sem=s_recv.at[place - 1], device_id={"dp": sibling}, device_id_type=MESH,
+            )
+
+        barrier = pltpu.get_barrier_semaphore()
+        for to in ({"tensor": near_x}, {"tensor": near_y}, {"dp": sibling}):
+            pl.semaphore_signal(barrier, inc=1, device_id=to, device_id_type=MESH)
+        pl.semaphore_wait(barrier, 3)
+        piece(0, 1, 0, near_x).start()
+        piece(0, 2, 1, near_y).start()
+        piece(0, 1, 1, near_x).start()
+        piece(0, 2, 0, near_y).start()
+        ow_all[0] = ow[:, moved:]
+    else:
+        out_ref, queries, keys, values, scores, begin_ref = refs[6:]
+    rows = x_ref.shape[0]
     lane = lax.broadcasted_iota(jnp.int32, (1, LANES), 1)
+    former = (lane % HD) < HD // 2
+    low = lane < HD
+
+    def rotated(tile, cos_table, sin_table):
+        swapped = jnp.where(
+            former, -pltpu.roll(tile, LANES - HD // 2, 1), pltpu.roll(tile, HD // 2, 1)
+        )
+        return tile * cos_table + swapped * sin_table
+
     index = lax.broadcasted_iota(jnp.int32, (rows, LANES), 0)
     begins = jnp.zeros((rows, LANES), jnp.int32)
     start = jnp.int32(0)
@@ -467,62 +516,8 @@
     steps_float = (lane % (HD // 2)).astype(F32)
     inverse = jnp.exp(steps_float * (-2.0 * math.log(10000.0) / HD))
     angles = (PLEN + index - begins).astype(F32) * inverse
-    cos_ref[...] = jnp.cos(angles)
-    sin_ref[...] = jnp.sin(angles)
-
-
-def attention_kernel(heads, parts, *refs):
-    (x_ref, wq_ref, wk_ref, wv_ref, cos_ref, sin_ref, begin_ref, kv_ref) = refs[:8]
-    if parts == 4:
-        ow, out_ref, ow_all, queries, keys, values, scores, w_send, w_recv, s_send, s_recv = refs[8:]
-        me = lax.axis_index("tensor")
-        group = lax.axis_index("dp")
-        core = group % 2
-        sibling = group + 1 - 2 * core
-        near_x, near_y = me + 1 - 2 * (me % 2), lax.rem(me + 2, parts)
-        quarter, moved = ow.shape[0] // 4, ow_all.shape[2]
-
-        def piece(src, place, half, to):
-            at = pl.ds((2 * core + half) * quarter, quarter)
-            return pltpu.make_async_remote_copy(
-                src_ref=ow.at[at, pl.ds(moved, moved)] if src == 0 else ow_all.at[src, at],
-                dst_ref=ow_all.at[place, at],
-                send_sem=w_send.at[2 * place + half - 2],
-                recv_sem=w_recv.at[2 * place + half - 2],
-                device_id={"tensor": to},
-                device_id_type=MESH,
-            )
-
-        def share(place):
-            ref = ow_all.at[place, pl.ds(2 * core * quarter, 2 * quarter)]
-            return pltpu.make_async_remote_copy(
-                src_ref=ref, dst_ref=ref, send_sem=s_send.at[place - 1],
-                recv_sem=s_recv.at[place - 1], device_id={"dp": sibling}, device_id_type=MESH,
-            )
-
-        barrier = pltpu.get_barrier_semaphore()
-        for to in ({"tensor": near_x}, {"tensor": near_y}, {"dp": sibling}):
-            pl.semaphore_signal(barrier, inc=1, device_id=to, device_id_type=MESH)
-        pl.semaphore_wait(barrier, 3)
-        piece(0, 1, 0, near_x).start()
-        piece(0, 2, 1, near_y).start()
-        piece(0, 1, 1, near_x).start()
-        piece(0, 2, 0, near_y).start()
-        ow_all[0] = ow[:, moved:]
-    else:
-        out_ref, queries, keys, values, scores = refs[8:]
-    rows = x_ref.shape[0]
-    lane = lax.broadcasted_iota(jnp.int32, (1, LANES), 1)
-    former = (lane % HD) < HD // 2
-    low = lane < HD
-
-    def rotated(tile, cos_table, sin_table):
-        swapped = jnp.where(
-            former, -pltpu.roll(tile, LANES - HD // 2, 1), pltpu.roll(tile, HD // 2, 1)
-        )
-        return tile * cos_table + swapped * sin_table
-
-    cos_table, sin_table = cos_ref[...], sin_ref[...]
+    cos_table, sin_table = jnp.cos(angles), jnp.sin(angles)
+
     x = x_ref[...]
     mapped = jnp.dot(x, wq_ref[...], preferred_element_type=F32)
     for h in range(heads):
@@ -624,25 +619,18 @@
     rows = x.shape[0]
     total = PLEN + rows
     block = 256 if rows % 256 == 0 else rows
-    table = jax.ShapeDtypeStruct((rows, LANES), F32)
-    tables = pl.pallas_call(
-        table_kernel,
-        out_shape=[table, table, jax.ShapeDtypeStruct((rows, LANES), jnp.int32)],
-        in_specs=[SMEM],
-        out_specs=[VMEM] * 3,
-        name="tables",
-    )(lengths)
     columns = pl.BlockSpec((wq.shape[0], LANES), lambda i: (0, tile()))
     whole = lambda shape: pl.BlockSpec(shape, lambda i: (0,) * len(shape))
     shapes = [jax.ShapeDtypeStruct((rows, (heads + 1) // 2 * LANES), BF16)]
-    operands = [x, wq, key_weight, value_weight, *tables, kv]
+    operands = [x, wq, key_weight, value_weight, lengths, kv]
     specs = [whole(x.shape), whole(wq.shape), columns, columns]
-    specs += [whole(t.shape) for t in tables] + [whole(kv.shape)]
+    specs += [SMEM, whole(kv.shape)]
     scratch = [
         pltpu.VMEM((heads, rows, LANES), BF16),
         pltpu.VMEM((total, LANES), BF16),
         pltpu.VMEM((total, LANES), BF16),
         pltpu.VMEM((2, block, total), F32),
+        pltpu.VMEM((rows, LANES), jnp.int32),
     ]
     params = dict(vmem_limit_bytes=52 * MIB)
     out_specs = [whole(shapes[0].shape)]

time: 132 us -> 127 us (0.962)
  local copies, waits for them, and re-layouts: 3.65 us -> 0.82 us
    unnamed x9, local copies, waits for them, and re-layouts: 3.65 us -> 0.82 us
    pallas_call x1 -> x0, Pallas kernels: 2.62 us -> none  [attention(): pl.pallas_call(table_kernel, out_shape=[table, table, jax.ShapeDtypeStruc...]
where the time goes in v6:
time: 127 us
  Pallas kernels  124 us (98%)
  other arithmetic  1.68 us (1%)
    pallas_call x1, Pallas kernels, gather(): pl.pallas_call(functools.partial(gather_kernel, parts, chips, width, sub)...  55.8 us
    pallas_call x1, Pallas kernels, mlp_square(): pl.pallas_call(mlp_square_kernel, out_shape=jax.ShapeDtypeStruct((rows, m...  45.7 us
    pallas_call x1, Pallas kernels, attention(): pl.pallas_call(functools.partial(attention_kernel, heads, parts), grid=(1...  22 us

profile of v6, /device:TPU:0, one launch (start us, length us, event | category | flops | bytes accessed | tf_op | source)
XLA Modules:
  0.0 127.0 jit_solution(8214008754647564432)
XLA Ops:
  0.0 0.8 select_reduce_fusion.1
  0.8 0.1 compare_and_fusion.1
  0.9 0.2 fusion
  1.0 0.6 reduce_max.19
  2.3 0.0 copy-start
  2.4 0.0 copy-start.1
  2.4 56.0 %conditional.1 = (bf16[512,2048]{1,0:T(8,128)(2,1)S(1)}, bf16[4096,128]{1,0:T(8,128)(2,1)}, bf16[4,256,1024]{2,1,0:T(8,128)(2,1)}) conditional(s32[]{:T(128)} %convert_element_type.7, (s32[8]{0:T(128)}, bf16[128,2048]{1,0:T(8,128)(2,1)}, bf16[1024,512]{1,0:T(8,128)(2,1)}, bf16[256,2048]{1,0:T(8,128)(2,1)}) %tuple.13, (s32[8]{0:T(128)}, ...), branch_computations={%region_4.5_spmd, %region_5.6_spmd} | conditional | bytes 24 | solution.py:971
  2.4 55.8 %gather.3 = (bf16[4,128,2048]{2,1,0:T(8,128)(2,1)S(1)}, bf16[16,256,128]{2,1,0:T(8,128)(2,1)}, bf16[4,256,1024]{2,1,0:T(8,128)(2,1)}) custom-call(s32[8]{0:T(128)} %get-tuple-element.28.refs_0_, bf16[128,2048]{1,0:T(8,128)(2,1)} %get-tuple-element.29.refs_1_, bf16[1024,512]{1,0:T(8,128)(2,1)} %get-tuple-element.30.refs_2_, ...), custom_call_target="tpu_custom_call" | custom-call | tf_op jit(solution)/shard_map/cond/branch_1_fun/gather/pallas_call | solution.py:431
  58.4 0.0 copy-done
  58.4 0.0 copy-done.1
  58.4 0.0 copy-start.2
  58.4 0.0 copy-start.3
  58.5 22.0 %attention.1 = (bf16[512,256]{1,0:T(8,128)(2,1)S(1)}, bf16[4,256,1024]{2,1,0:T(8,128)(2,1)}) custom-call(bf16[512,2048]{1,0:T(8,128)(2,1)S(1)} %get-tuple-element.40.refs_0_, bf16[2048,256]{1,0:T(8,128)(2,1)S(1)} %copy-done, bf16[2048,256]{1,0:T(8,128)(2,1)} %refs_2_.1, bf16[2048,256]{1,0:T(8,128)(2,1)} %refs_3_.1, s32[1,8]{1,0:T(1,128)S(1)} %copy-done.1, ...), custom_call_target="tpu_custom_call" | custom-call | tf_op jit(solution)/shard_map/attention/pallas_call | solution.py:644
  80.4 0.0 copy-done.2
  80.5 0.0 copy-done.3
  80.5 45.7 %mlp.1 = bf16[128,2048]{1,0:T(8,128)(2,1)S(1)} custom-call(bf16[512,256]{1,0:T(8,128)(2,1)S(1)} %get-tuple-element.42.att, bf16[4,256,1024]{2,1,0:T(8,128)(2,1)S(1)} %copy-done.3, bf16[4,256,1024]{2,1,0:T(8,128)(2,1)} %get-tuple-element.44.out_r, bf16[128,2048]{1,0:T(8,128)(2,1)S(1)} %copy-done.2, bf16[2,2048,1280]{2,1,0:T(8,128)(2,1)} %gate_up.1, ...), custom_call_target="tpu_custom_call" | custom-call | tf_op jit(solution)/shard_map/mlp/pallas_call | solution.py:899
  126.2 0.8 copy.20
  (1 shorter events, 0.0 us)
Async XLA Ops:
  2.3 56.1 %copy-start = (bf16[2048,256]{1,0:T(8,128)(2,1)S(1)}, bf16[2048,256]{1,0:T(8,128)(2,1)}, u32[]{:S(2)}) copy-start(bf16[2048,256]{1,0:T(8,128)(2,1)} %refs_1_.1) | copy-start | bytes 3145732
  2.4 56.1 %copy-start.1 = (s32[1,8]{1,0:T(1,128)S(1)}, s32[1,8]{1,0:T(1,128)}, u32[]{:S(2)}) copy-start(s32[1,8]{1,0:T(1,128)} %refs_4_.1) | copy-start | bytes 100
  58.4 22.0 %copy-start.2 = (bf16[128,2048]{1,0:T(8,128)(2,1)S(1)}, bf16[128,2048]{1,0:T(8,128)(2,1)}, u32[]{:S(2)}) copy-start(bf16[128,2048]{1,0:T(8,128)(2,1)} %tokens.1) | copy-start | bytes 1572868
  58.4 22.0 %copy-start.3 = (bf16[4,256,1024]{2,1,0:T(8,128)(2,1)S(1)}, bf16[4,256,1024]{2,1,0:T(8,128)(2,1)}, u32[]{:S(2)}) copy-start(bf16[4,256,1024]{2,1,0:T(8,128)(2,1)} %get-tuple-element.43.out_l) | copy-start | bytes 6291460
